TPU v7x, 512 devices: a whole 4x8x8 slice. The times are simulated.
512 devices in a mesh: ka: 128 (over y, z, core), pair: 4 (over x).
Axes of the slice: x: 4, y: 8, z: 8, core: 2. Of those that a mesh axis runs over, the one named last changes fastest.
Arguments:
- kkr_matrix: bfloat16 [512, 2, 256, 256], P('ka'), may hold values from -0.125 to 0.125
- kpoint_grid: int32 [512, 3], P('ka'), may hold values from 0 to 15
- lattice: int32 [8, 3], replicated, may hold values from -3 to 3, as said below
- delta_t: bfloat16 [4, 2, 256, 256], replicated, may hold values from -0.25 to 0.25
- pair_count: int32 [128], replicated, may hold values from 1 to 8, as said below
- pair_route: int32 [128, 8], replicated, may hold values from 0 to 7
- species: int32 [128, 8], replicated, may hold values from 0 to 3
Outputs:
- host_blocks: float32 [2048, 512], P('ka', 'pair')
- cluster_blocks: bfloat16 [1024, 256, 512], P('ka', None, 'pair')
Inputs may be any that keep to these rules, and one draw needn't show every extreme that they name: Distinct lattice vectors, each component from -3 to 3. `pair_count`: every owner holds at least one pair; some owner, drawn from the seed, fills all 8 slots; slots at or past an owner's count are ignored.
All inputs are finite; a program needn't handle non-finite values.
Results may differ from a plain program's by a relative error of at most 0.0049.
Values may be sent and summed in bfloat16 or wider, within the bound.
No kernel may reach another device: no remote copies, remote signals or barrier semaphores. Data moves between devices by JAX's collectives and lax.ppermute only.
A program may use at most 64 MiB of HBM per device.

v0:
```python
import math

import jax
import jax.numpy as jnp
from jax import lax
from jax.sharding import PartitionSpec as P

ITERS = 6
KG = 16


PRECISE = lax.Precision.HIGHEST


def phases(kpoint_grid, lattice):
    turn_index = jnp.mod(jnp.dot(kpoint_grid, lattice.T), KG).astype(jnp.float32)
    angles = turn_index * (2.0 * math.pi / KG)
    return (jnp.cos(angles), jnp.sin(angles))


def per_device(kkr_matrix, kpoint_grid, lattice, delta_t, pair_count, pair_route, species):
    pieces = lax.axis_size("pair")
    site_order = kkr_matrix.shape[2]
    columns = site_order // pieces
    first_column = lax.axis_index("pair") * columns
    kpoints = kkr_matrix.shape[0]
    lattice_count = lattice.shape[0]
    weight_scale = math.sqrt(site_order / (kpoints * lax.axis_size("ka")))
    cosine, sine_part = phases(kpoint_grid, lattice)

    def solve_one(matrix):
        stacked = matrix.astype(jnp.float32).reshape(2 * site_order, site_order)
        window = lax.dynamic_slice_in_dim(stacked, first_column, columns, 1)
        initial = jnp.concatenate([window[:site_order], window[site_order:]], axis=1)
        current = initial
        for iteration in range(ITERS - 1):
            products = jnp.dot(stacked, current, precision=PRECISE)
            upper_half = products[:site_order]
            lower_half = products[site_order:]
            turned = jnp.concatenate([-lower_half[:, columns:], lower_half[:, :columns]], axis=1)
            current = initial + upper_half + turned
        return current

    solved = lax.map(solve_one, kkr_matrix)
    shaped = solved.reshape(kpoints, site_order, 2, columns)
    weights = (
        jnp.stack([jnp.stack([cosine, sine_part], -1), jnp.stack([-sine_part, cosine], -1)], 2)
        * weight_scale
    )
    own_rows = site_order * lattice_count // lax.axis_size("ka")
    summed = jnp.einsum("krab,kiac->irbc", weights, shaped, precision=PRECISE)
    host_rows = lax.psum_scatter(
        summed.reshape(own_rows * lax.axis_size("ka"), 2 * columns),
        "ka",
        scatter_dimension=0,
        tiled=True,
    )
    owners = lax.axis_size("ka")
    slot_count = pair_route.shape[1]
    kind_count = delta_t.shape[0]
    local_rows = host_rows.shape[0] // lattice_count
    alive_mask = (
        (jnp.arange(slot_count)[None, :] < pair_count[:, None]).astype(jnp.bfloat16).reshape(-1)
    )
    flat_route = pair_route.reshape(-1)
    rounded = host_rows.astype(jnp.bfloat16)
    real_window = lax.dynamic_slice_in_dim(delta_t[:, 0], first_column, columns, 2).reshape(
        kind_count, pieces, columns, columns
    )
    imag_window = lax.dynamic_slice_in_dim(delta_t[:, 1], first_column, columns, 2).reshape(
        kind_count, pieces, columns, columns
    )
    top_rows = jnp.concatenate([real_window, imag_window], -1)
    bottom = jnp.concatenate([-imag_window, real_window], -1)
    coupling = jnp.stack([top_rows, bottom], 2).reshape(kind_count, 2 * site_order, 2 * columns)
    ordered = rounded.reshape(local_rows, lattice_count, 2 * columns).transpose(1, 0, 2)
    outgoing = jnp.take(ordered, flat_route, axis=0) * alive_mask[:, None, None]
    outgoing = outgoing.reshape(owners, slot_count, local_rows, 2 * columns)
    arrived = lax.all_to_all(outgoing, "ka", split_axis=0, concat_axis=2, tiled=True)
    blocks = lax.all_gather(arrived, "pair", axis=3, tiled=True)
    own_species = lax.dynamic_slice_in_dim(species, lax.axis_index("ka"), 1, 0)[0]
    chosen = jnp.take(coupling, own_species, axis=0)
    product = jnp.einsum("sbc,sco->sbo", blocks[0], chosen, preferred_element_type=jnp.float32)
    cluster = product.astype(jnp.bfloat16)
    return (host_rows, cluster)


def solution(mesh):
    in_specs = (P("ka", None, None, None), P("ka", None), P(), P(), P(), P(), P())
    out_specs = (P("ka", "pair"), P("ka", None, "pair"))
    return jax.shard_map(
        per_device, mesh=mesh, in_specs=in_specs, out_specs=out_specs, check_vma=False
    )
```

profile of v0, /device:TPU:1, one launch (start us, length us, event | category | flops | bytes accessed | tf_op | source)
XLA Modules:
  0.0 308.9 jit_solution(8396301717278981023)
XLA Ops:
  7.3 13.6 %while.12 = (s32[]{:T(128)}, f32[4,256,128]{1,2,0:T(8,128)S(1)}, bf16[4,2,256,256]{3,2,1,0:T(8,128)(2,1)}, s32[]{:T(128)}, s32[]{:T(128)}) while((s32[]{:T(128)}, f32[4,256,128]{1,2,0:T(8,128)S(1)}, bf16[4,2,256,256]{3,2,1,0:T(8,128)(2,1)}, s32[]{:T(128)}, s32[]{:T(128)}) %tuple.57), condition=%wide.region_1.2_spmd, body=%wide.region_0.1_spmd.sunk | while | flops 1007403008 | bytes 7209041 | solution.py:44
  7.3 1.0 constant_dynamic-slice_fusion.6
  8.3 0.1 constant_dynamic-slice_fusion.7
  8.5 0.4 fusion.93
  8.9 0.4 fusion.94
  9.3 0.4 fusion.95
  9.8 0.4 fusion.96
  10.2 0.4 fusion.97
  10.7 1.0 constant_dynamic-slice_fusion.6
  11.6 0.1 constant_dynamic-slice_fusion.7
  11.9 0.4 fusion.93
  12.3 0.4 fusion.94
  12.7 0.4 fusion.95
  13.2 0.4 fusion.96
  13.6 0.4 fusion.97
  14.1 1.0 constant_dynamic-slice_fusion.6
  15.0 0.1 constant_dynamic-slice_fusion.7
  15.3 0.4 fusion.93
  15.7 0.4 fusion.94
  16.1 0.4 fusion.95
  16.6 0.4 fusion.96
  17.0 0.4 fusion.97
  17.5 1.0 constant_dynamic-slice_fusion.6
  18.4 0.1 constant_dynamic-slice_fusion.7
  18.7 0.4 fusion.93
  19.1 0.4 fusion.94
  19.5 0.4 fusion.95
  19.9 0.4 fusion.96
  20.4 0.4 fusion.97
  20.9 0.2 fusion.57
  21.1 1.3 convolution_bitcast_fusion
  22.4 1.9 copy.38
  24.3 2.1 reshape.121
  26.5 0.1 copy.41
  26.6 0.1 reshape.123
  26.8 0.1 copy.39
  27.0 198.9 %reduce-scatter.2.cloned.1.call-done = f32[16,128]{1,0:T(8,128)} async-done(((f32[2048,128]{1,0:T(8,128)}), f32[16,128]{1,0:T(8,128)}) %reduce-scatter.2.cloned.1.call-update) | async-done | bytes 8208 | tf_op jit(solution)/shard_map/reduce_scatter | solution.py:52
  225.9 0.7 convert_bitcast_fusion
  226.6 3.7 %gather_fusion = bf16[1024,2,128]{2,1,0:T(2,128)(2,1)S(1)} fusion(bf16[8,2,128]{2,1,0:T(2,128)(2,1)S(1)} %bitcast.89, s32[1024]{0:T(1024)S(1)} %broadcast_clamp_fusion), kind=kCustom, calls=%fused_computation | custom fusion | bytes 1052672 | tf_op jit(solution)/shard_map/jit(_take)/gather | solution.py:77
  230.3 0.3 fusion.40
  230.8 34.2 %all_to_all.18 = bf16[128,8,2,128]{3,1,2,0:T(8,128)(2,1)S(1)} all-to-all(bf16[128,8,2,128]{3,1,2,0:T(8,128)(2,1)S(1)} %copy.43), channel_id=1, replica_groups=mesh['ka'=128,'pair'=4] {'ka'}, dimensions={0} | all-to-all | bytes 1048576 | tf_op jit(solution)/shard_map/all_to_all | solution.py:79
  264.9 1.2 copy.44
  266.2 0.2 constant_dynamic-slice_fusion.2
  266.6 0.2 dynamic-slice_reduce_fusion
  266.8 0.3 maximum_bitcast_fusion
  267.1 0.7 gather_fusion.1
  267.9 31.0 %all-gather.2.cloned.1.call-done = bf16[1,8,256,512]{3,2,1,0:T(8,128)(2,1)} async-done(((bf16[1,8,256,128]{3,2,1,0:T(8,128)(2,1)}), bf16[1,8,256,512]{3,2,1,0:T(8,128)(2,1)}) %all-gather.2.cloned.1.call-update) | async-done | bytes 2097168 | tf_op jit(solution)/shard_map/all_gather | solution.py:80
  298.9 3.2 %fusion.35 = bf16[8,256,128]{2,1,0:T(8,128)(2,1)} fusion(bf16[1,8,256,512]{3,2,1,0:T(8,128)(2,1)} %all-gather.2.cloned.1.call-done, bf16[8,512,128]{2,1,0:T(8,128)(2,1)S(1)} %gather_fusion.1, pred[8]{0:T(512)(128)(4,1)S(1)} %compare_and_fusion.1), kind=kOutput, calls=%fused_computation.47 | convolution fusion | flops 269221888 | bytes 3670024 | tf_op jit(solution)/shard_map/sbc,sco->sbo/dot_general | solution.py:83
  (62 shorter events, 1.4 us)
Async XLA Ops:
  7.2 259.4 %copy-start = (s32[128,8]{0,1:T(8,128)S(1)}, s32[128,8]{0,1:T(8,128)}, u32[]{:S(2)}) copy-start(s32[128,8]{0,1:T(8,128)} %param.15) | copy-start | bytes 12292
  7.2 218.7 %reduce-scatter.2.cloned.1.call-start = ((), (), s32[]{:S(2)}) async-start(), calls=%async_computation.2 | async-start | bytes 1056768 | tf_op jit(solution)/shard_map/reduce_scatter | solution.py:52
  7.2 13.6 %copy-start.4 = (s32[4,3]{1,0:T(4,128)S(1)}, s32[4,3]{1,0:T(4,128)}, u32[]{:S(2)}) copy-start(s32[4,3]{1,0:T(4,128)} %param.10) | copy-start | bytes 148
  7.3 13.6 %copy-start.5 = (s32[8,3]{0,1:T(4,128)S(1)}, s32[8,3]{0,1:T(4,128)}, u32[]{:S(2)}) copy-start(s32[8,3]{0,1:T(4,128)} %param.11) | copy-start | bytes 292
  24.3 2.2 copy-start.2
  24.3 2.6 copy-start.3
  26.5 272.4 %all-gather.2.cloned.1.call-start = ((), (), s32[]{:S(2)}) async-start(), calls=%async_computation.3 | async-start | bytes 2621440 | tf_op jit(solution)/shard_map/all_gather | solution.py:80
  230.6 35.5 %copy-start.1 = (bf16[4,2,256,256]{3,2,1,0:T(8,128)(2,1)S(1)}, bf16[4,2,256,256]{3,2,1,0:T(8,128)(2,1)}, u32[]{:S(2)}) copy-start(bf16[4,2,256,256]{3,2,1,0:T(8,128)(2,1)} %param.12) | copy-start | bytes 3145732
Sparse Core Ops, SparseCore 0:
  26.6 199.2 reduce-scatter.1
  266.3 32.5 all-gather.1
where the time goes:
time: 309 us
  waiting for transfers between devices  230 us (74%)
  blocking collectives  34.2 us (11%)
  local copies, waits for them, and re-layouts  15.4 us (5%)
  between operations  14.3 us (5%)
  matrix products  12.6 us (4%)
    reduce_scatter x1, waiting for transfers between devices, per_device(): lax.psum_scatter(summed.reshape(own_rows * lax.axis_size('ka'), 2 * colum...  199 us
    all_to_all x1, blocking collectives, per_device(): lax.all_to_all(outgoing, 'ka', split_axis=0, concat_axis=2, tiled=True)  34.2 us
    all_gather x1, waiting for transfers between devices, per_device(): blocks = lax.all_gather(arrived, 'pair', axis=3, tiled=True)  31 us
    dot_general x20, matrix products, solve_one(): products = jnp.dot(stacked, current, precision=PRECISE)  7.95 us
  transfers between devices with their start and end apart: 2, of which 2 were waited for; matrix products, arithmetic and copies ran while one was open for 1% of the time, Pallas kernels for 0%

commit v1 on v0

v1 whole, which is shorter than its diff:
```python
import functools
import math

import jax
import jax.numpy as jnp
import numpy as np
from jax import lax
from jax.experimental import pallas as pl
from jax.experimental.pallas import tpu as pltpu
from jax.sharding import Mesh
from jax.sharding import PartitionSpec as P

ITERS = 6
KG = 16
LANES = 128
CHIPS = ("y", "z")
CORES = ("c", "pair")
F32 = jnp.float32
BF16 = jnp.bfloat16


def dot(a, b):
    return jnp.dot(a, b, preferred_element_type=F32)


def turn_tables():
    angles = np.arange(KG) * (2.0 * math.pi / KG)
    tables = []
    for values in (np.cos(angles), np.sin(angles)):
        values = values.astype(np.float32)
        high = values.astype(jnp.bfloat16).astype(np.float32)
        tables += [high, (values - high).astype(jnp.bfloat16).astype(np.float32)]
    return tables


def solve_kernel(spot, grid, lattice, matrix, out, wide):
    kpoints, _, order, _ = matrix.shape
    own = order // 4
    chunk = out.shape[0] // own
    row = lax.broadcasted_iota(jnp.int32, (own, order), 0)
    col = lax.broadcasted_iota(jnp.int32, (own, order), 1)
    pick = jnp.where(col == row * 4 + spot[0], 1.0, 0.0).astype(BF16)
    first = [[dot(pick, matrix[k, part]) for part in range(2)] for k in range(kpoints)]
    now = [list(pair) for pair in first]
    for step in range(ITERS - 1):
        for k in range(kpoints):
            re, im = now[k]
            re_high, im_high = re.astype(BF16), im.astype(BF16)
            parts = [re_high, im_high]
            if step > 0:
                parts.append((re - re_high.astype(F32)).astype(BF16))
                parts.append((im - im_high.astype(F32)).astype(BF16))
            left = jnp.concatenate(parts, axis=0)
            u = dot(left, matrix[k, 0])
            v = dot(left, matrix[k, 1])
            if step > 0:
                u = u[: 2 * own] + u[2 * own :]
                v = v[: 2 * own] + v[2 * own :]
            now[k] = [
                first[k][0] + u[:own] - v[own:],
                first[k][1] + v[:own] + u[own:],
            ]
    for k in range(kpoints):
        for part in range(2):
            for half in range(order // LANES):
                place = (k * 2 + part) * (order // LANES) + half
                wide[pl.ds(place, own, stride=chunk), :] = now[k][part][
                    :, half * LANES : (half + 1) * LANES
                ]
    vectors = lattice.shape[0]
    lane = lax.broadcasted_iota(jnp.int32, (8, LANES), 1)
    turn = jnp.zeros((8, LANES), jnp.int32)
    for r in range(vectors):
        for k in range(kpoints):
            m = (
                grid[k, 0] * lattice[r, 0]
                + grid[k, 1] * lattice[r, 1]
                + grid[k, 2] * lattice[r, 2]
            ) & (KG - 1)
            here = ((lane // (4 * vectors)) == k) & ((lane & (vectors - 1)) == r)
            turn = jnp.where(here, m, turn)
    kind = (lane // vectors) & 3
    phase = jnp.zeros((8, LANES), F32)
    for which, table in enumerate(turn_tables()):
        for m in range(KG):
            phase = jnp.where((kind == which) & (turn == m), float(table[m]), phase)
    phase = jnp.broadcast_to(phase[:1], (own, LANES))
    wide[pl.ds(chunk - 2, own, stride=chunk), :] = phase
    wide[pl.ds(chunk - 1, own, stride=chunk), :] = jnp.zeros((own, LANES), F32)
    out[...] = wide[...].astype(BF16)


def phase_kernel(kpoints, vectors, rows, out, wide):
    chunk = 2 + 4 * kpoints
    sources = rows.shape[0] // chunk
    wide[...] = rows[...].astype(F32)
    info = wide[pl.ds(chunk - 2, sources, stride=chunk), :]
    info = jnp.transpose(info).astype(BF16)
    total = jnp.zeros((4 * vectors, 4 * LANES), F32)
    for k in range(kpoints):
        block = [wide[pl.ds(k * 4 + q, sources, stride=chunk), :] for q in range(4)]
        block = jnp.concatenate(block, axis=1).astype(BF16)
        total = total + dot(info[k * 4 * vectors : (k + 1) * 4 * vectors], block)
    cosine = total[:vectors] + total[vectors : 2 * vectors]
    sine = total[2 * vectors : 3 * vectors] + total[3 * vectors :]
    half = 2 * LANES
    re = cosine[:, :half] - sine[:, half:]
    im = cosine[:, half:] + sine[:, :half]
    both = jnp.concatenate([re, im], axis=1)
    out[...] = jnp.broadcast_to(both[None], out.shape)


def coupling_kernel(spot, delta, out):
    kinds, _, order, _ = delta.shape
    row = lax.broadcasted_iota(jnp.int32, (order, LANES), 0)
    col = lax.broadcasted_iota(jnp.int32, (order, LANES), 1)
    half = LANES // 2
    left = ((col < half) & (row == spot[0] * half + col)).astype(F32).astype(BF16)
    right = ((col >= half) & (row == spot[0] * half + col - half)).astype(F32).astype(BF16)
    for s in range(kinds):
        re, im = delta[s, 0], delta[s, 1]
        out[:order, s * LANES : (s + 1) * LANES] = (dot(re, left) + dot(im, right)).astype(BF16)
        out[order:, s * LANES : (s + 1) * LANES] = (dot(re, right) - dot(im, left)).astype(BF16)


def product_kernel(scale, spot, parts, coupling, chosen, host, out, wide, sums):
    vectors = parts.shape[1]
    order = parts.shape[2] // 2
    half = LANES // 2
    for q in range(4):
        sums[q * vectors : (q + 1) * vectors, :] = (parts[q] + parts[4 + q]) * scale
    own = pl.multiple_of(spot[1] * (2 * vectors), 2 * vectors)
    at = pl.multiple_of((spot[0] // 2) * LANES, LANES)
    re = sums[pl.ds(own, 2 * vectors), pl.ds(at, LANES)]
    im = sums[pl.ds(own, 2 * vectors), pl.ds(order + at, LANES)]
    lane = lax.broadcasted_iota(jnp.int32, re.shape, 1)
    odd = (spot[0] & 1) == 1
    re = jnp.where(odd, pltpu.roll(re, half, 1), re)
    im = jnp.where(odd, im, pltpu.roll(im, half, 1))
    host[...] = jnp.where(lane < half, re, im)
    product = dot(sums[...].astype(BF16), coupling[...])
    kinds = coupling.shape[1] // LANES
    table = jnp.concatenate(
        [
            jnp.concatenate(
                [
                    product[q * vectors : (q + 1) * vectors, s * LANES : (s + 1) * LANES]
                    for q in range(4)
                ],
                axis=1,
            )
            for s in range(kinds)
        ],
        axis=0,
    ).astype(BF16)
    picked = dot(chosen[...], table)
    for q in range(4):
        wide[pl.ds(q, picked.shape[0], stride=4), :] = picked[:, q * LANES : (q + 1) * LANES]
    out[...] = wide[...].astype(BF16)


VMEM = pl.BlockSpec(memory_space=pltpu.VMEM)
SMEM = pl.BlockSpec(memory_space=pltpu.SMEM)


def params():
    return pltpu.CompilerParams(vmem_limit_bytes=32 * 1024 * 1024)


def per_device(kkr_matrix, kpoint_grid, lattice, delta_t, pair_count, pair_route, species):
    chips = lax.axis_size(CHIPS)
    cores = lax.axis_size(CORES)
    pair = lax.axis_index("pair")
    core = lax.axis_index("c")
    spot = jnp.stack([pair, core]).astype(jnp.int32)
    order = kkr_matrix.shape[2]
    kpoints = kkr_matrix.shape[0]
    vectors = lattice.shape[0]
    slots = pair_route.shape[1]
    kinds = delta_t.shape[0]
    scale = math.sqrt(order / (kpoints * chips * lax.axis_size("c")))
    chunk = 4 * kpoints + 2
    length = chips * chunk

    outgoing = pl.pallas_call(
        solve_kernel,
        out_shape=jax.ShapeDtypeStruct((length, LANES), BF16),
        in_specs=[SMEM, SMEM, SMEM, VMEM],
        out_specs=VMEM,
        scratch_shapes=[pltpu.VMEM((length, LANES), F32)],
        compiler_params=params(),
        name="solve",
    )(spot, kpoint_grid, lattice, kkr_matrix)
    outgoing = outgoing.reshape(chips, chunk // 2, 2, LANES)
    arrived = lax.all_to_all(outgoing, CHIPS, split_axis=0, concat_axis=0, tiled=True)

    coupling = pl.pallas_call(
        coupling_kernel,
        out_shape=jax.ShapeDtypeStruct((2 * order, kinds * LANES), BF16),
        in_specs=[SMEM, VMEM],
        out_specs=VMEM,
        compiler_params=params(),
        cost_estimate=pl.CostEstimate(
            flops=16 * kinds * order * order * LANES, bytes_accessed=2 << 20, transcendentals=0
        ),
        name="coupling",
    )(spot, delta_t)
    alive = jnp.arange(slots)[None, :] < pair_count[:, None]
    combo = jnp.where(alive, species * vectors + pair_route, -1)
    combo = lax.dynamic_index_in_dim(combo.reshape(chips, 2, slots), core, 1, keepdims=False)
    chosen = (combo.reshape(-1, 1) == jnp.arange(kinds * vectors)[None, :]).astype(BF16)

    parts = pl.pallas_call(
        functools.partial(phase_kernel, kpoints, vectors),
        out_shape=jax.ShapeDtypeStruct((cores, vectors, 2 * order), F32),
        in_specs=[VMEM],
        out_specs=VMEM,
        scratch_shapes=[pltpu.VMEM((length, LANES), F32)],
        compiler_params=params(),
        name="phase_sum",
    )(arrived.reshape(length, LANES))
    parts = lax.all_to_all(parts, CORES, split_axis=0, concat_axis=0, tiled=True)

    host_rows, sent = pl.pallas_call(
        functools.partial(product_kernel, scale),
        out_shape=(
            jax.ShapeDtypeStruct((2 * vectors, LANES), F32),
            jax.ShapeDtypeStruct((chips * slots * 4, LANES), BF16),
        ),
        in_specs=[SMEM, VMEM, VMEM, VMEM],
        out_specs=(VMEM, VMEM),
        scratch_shapes=[
            pltpu.VMEM((chips * slots * 4, LANES), F32),
            pltpu.VMEM((4 * vectors, 2 * order), F32),
        ],
        compiler_params=params(),
        name="product",
    )(spot, parts, coupling, chosen)
    sent = sent.reshape(chips, slots * 4, LANES)
    got = lax.all_to_all(sent, CHIPS, split_axis=0, concat_axis=0, tiled=True)
    cluster = got.reshape(chips, slots, 4, LANES).transpose(1, 0, 2, 3)
    return (host_rows, cluster.reshape(slots, order, LANES))


def solution(mesh):
    fine = Mesh(mesh.devices.reshape(8, 8, 2, 4), ("y", "z", "c", "pair"))
    ka = ("y", "z", "c")
    in_specs = (P(ka, None, None, None), P(ka, None), P(), P(), P(), P(), P())
    out_specs = (P(ka, "pair"), P(ka, None, "pair"))
    return jax.shard_map(
        per_device, mesh=fine, in_specs=in_specs, out_specs=out_specs, check_vma=False
    )
```

time: 309 us -> 75.9 us (0.25)
  the two profiles are of different devices: /device:TPU:1 before, /device:TPU:16 now
where the time goes in v1:
time: 75.9 us; the launch traced here: 75.5 us
  blocking collectives  24.6 us (32%)
  starting transfers between devices  20.9 us (28%)
  waiting for transfers between devices  18.4 us (24%)
  Pallas kernels  6.82 us (9%)
  local copies, waits for them, and re-layouts  3.89 us (5%)
    all_to_all x1, blocking collectives, per_device(): got = lax.all_to_all(sent, CHIPS, split_axis=0, concat_axis=0, tiled=True)  24.6 us
    all_to_all x1, starting transfers between devices, per_device(): lax.all_to_all(outgoing, CHIPS, split_axis=0, concat_axis=0, tiled=True)  16.6 us
    all_to_all x1, waiting for transfers between devices, per_device(): lax.all_to_all(outgoing, CHIPS, split_axis=0, concat_axis=0, tiled=True)  14.3 us
    all_to_all x1, starting transfers between devices, per_device(): lax.all_to_all(parts, CORES, split_axis=0, concat_axis=0, tiled=True)  4.3 us
    all_to_all x1, waiting for transfers between devices, per_device(): lax.all_to_all(parts, CORES, split_axis=0, concat_axis=0, tiled=True)  4.15 us
    pallas_call x1, Pallas kernels, per_device(): pl.pallas_call(solve_kernel, out_shape=jax.ShapeDtypeStruct((length, LANE...  3.07 us
    unnamed x15, local copies, waits for them, and re-layouts  2.6 us
    pallas_call x1, Pallas kernels, per_device(): pl.pallas_call(functools.partial(product_kernel, scale), out_shape=(jax.S...  1.57 us
  transfers between devices with their start and end apart: 2, of which 2 were waited for; matrix products, arithmetic and copies ran while one was open for 1% of the time, Pallas kernels for 2%

profile of v1, /device:TPU:16, one launch (start us, length us, event | category | flops | bytes accessed | tf_op | source)
XLA Modules:
  0.0 75.5 jit_solution(720564698430508501)
XLA Ops:
  0.6 0.0 copy-start.5
  0.6 0.7 copy-done.5
  1.3 0.1 copy.11.lattice
  1.4 0.0 copy-start.1
  1.4 0.1 pad_add_fusion.spot
  1.5 0.6 copy-done.1
  2.1 0.0 copy-start
  2.1 1.2 %copy-done = bf16[4,2,256,256]{3,2,1,0:T(8,128)(2,1)S(1)} copy-done((bf16[4,2,256,256]{3,2,1,0:T(8,128)(2,1)S(1)}, bf16[4,2,256,256]{3,2,1,0:T(8,128)(2,1)}, u32[]{:S(2)}) %copy-start) | copy-done | bytes 1048600
  3.3 0.0 copy-start.3
  3.3 0.0 copy-start.4
  3.3 0.0 copy-start.6
  3.3 3.1 %solve.1 = bf16[1152,128]{1,0:T(8,128)(2,1)} custom-call(s32[2]{0:T(128)S(1)} %pad_add_fusion.spot, s32[4,3]{1,0:T(4,128)S(1)} %copy-done.1, s32[8,3]{1,0:T(8,128)S(1)} %copy.11.lattice, bf16[4,2,256,256]{3,2,1,0:T(8,128)(2,1)S(1)} %copy-done), custom_call_target="tpu_custom_call" | custom-call | tf_op jit(solution)/shard_map/solve/pallas_call | solution.py:185
  6.4 0.0 copy-start.2
  6.4 16.6 %all-to-all-start = ((bf16[64,9,2,128]{3,2,1,0:T(2,128)(2,1)}), bf16[64,9,2,128]{3,2,1,0:T(2,128)(2,1)S(1)}, u32[]{:S(2)}, u32[]{:S(2)}) async-start(bf16[64,9,2,128]{3,2,1,0:T(2,128)(2,1)} %bitcast.2), calls=%async_computation | async-start | bytes 589824 | tf_op jit(solution)/shard_map/all_to_all | solution.py:195
  23.0 0.0 copy-done.3
  23.0 0.0 copy-done.4
  23.0 0.0 copy-done.6
  23.0 0.1 copy.12
  23.1 0.1 dynamic-slice_reduce_fusion
  23.2 0.1 eq.15
  23.3 14.3 %all-to-all-done = bf16[64,9,2,128]{3,2,1,0:T(2,128)(2,1)S(1)} async-done(((bf16[64,9,2,128]{3,2,1,0:T(2,128)(2,1)}), bf16[64,9,2,128]{3,2,1,0:T(2,128)(2,1)S(1)}, u32[]{:S(2)}, u32[]{:S(2)}) %all-to-all-start) | async-done | bytes 294944 | tf_op jit(solution)/shard_map/all_to_all | solution.py:195
  37.6 0.9 %phase_sum.1 = f32[8,8,512]{2,1,0:T(8,128)} custom-call(bf16[1152,128]{1,0:T(8,128)(2,1)S(1)} %bitcast.10), custom_call_target="tpu_custom_call" | custom-call | tf_op jit(solution)/shard_map/phase_sum/pallas_call | solution.py:213
  38.5 4.3 %all-to-all-start.1 = ((f32[8,8,512]{2,1,0:T(8,128)}), f32[8,8,512]{2,1,0:T(8,128)S(1)}, u32[]{:S(2)}, u32[]{:S(2)}) async-start(f32[8,8,512]{2,1,0:T(8,128)} %phase_sum.1), calls=%async_computation.1 | async-start | bytes 262144 | tf_op jit(solution)/shard_map/all_to_all | solution.py:222
  42.8 0.1 fusion.chosen
  43.0 0.0 copy-done.2
  43.0 1.2 %coupling.1 = bf16[512,512]{1,0:T(8,128)(2,1)S(1)} custom-call(s32[2]{0:T(128)S(1)} %pad_add_fusion.spot, bf16[4,2,256,256]{3,2,1,0:T(8,128)(2,1)S(1)} %copy-done.2), custom_call_target="tpu_custom_call" | custom-call | flops 536870912 | bytes 2097152 | tf_op jit(solution)/shard_map/coupling/pallas_call | solution.py:197
  44.2 4.2 %all-to-all-done.1.parts = f32[8,8,512]{2,1,0:T(8,128)S(1)} async-done(((f32[8,8,512]{2,1,0:T(8,128)}), f32[8,8,512]{2,1,0:T(8,128)S(1)}, u32[]{:S(2)}, u32[]{:S(2)}) %all-to-all-start.1) | async-done | bytes 131104 | tf_op jit(solution)/shard_map/all_to_all | solution.py:222
  48.4 1.6 %product.1 = (f32[16,128]{1,0:T(8,128)}, bf16[2048,128]{1,0:T(8,128)(2,1)S(1)}) custom-call(s32[2]{0:T(128)S(1)} %pad_add_fusion.spot, f32[8,8,512]{2,1,0:T(8,128)S(1)} %all-to-all-done.1.parts, bf16[512,512]{1,0:T(8,128)(2,1)S(1)} %coupling.1, bf16[512,32]{1,0:T(8,128)(2,1)S(1)} %fusion.chosen), custom_call_target="tpu_custom_call" | custom-call | tf_op jit(solution)/shard_map/product/pallas_call | solution.py:224
  50.0 24.6 %all_to_all.15 = bf16[64,32,128]{2,1,0:T(8,128)(2,1)S(1)} all-to-all(bf16[64,32,128]{2,1,0:T(8,128)(2,1)S(1)} %bitcast.11), channel_id=1, replica_groups=mesh['y'=8,'z'=8,'c'=2,'pair'=4] {'y','z'}, dimensions={0} | all-to-all | bytes 1048576 | tf_op jit(solution)/shard_map/all_to_all | solution.py:240
  74.5 1.0 %copy.13 = bf16[64,8,4,128]{3,2,0,1:T(4,128)(2,1)} copy(bf16[64,8,4,128]{3,2,1,0:T(4,128)(2,1)S(1)} %bitcast.12) | data formatting | bytes 1048576 | tf_op jit(solution)/shard_map/reshape | solution.py:241
  (1 shorter events, 0.0 us)
Async XLA Ops:
  0.6 0.7 copy-start.5
  1.4 0.7 copy-start.1
  2.1 1.2 %copy-start = (bf16[4,2,256,256]{3,2,1,0:T(8,128)(2,1)S(1)}, bf16[4,2,256,256]{3,2,1,0:T(8,128)(2,1)}, u32[]{:S(2)}) copy-start(bf16[4,2,256,256]{3,2,1,0:T(8,128)(2,1)} %matrix.1) | copy-start | bytes 3145732
  3.3 19.7 %copy-start.3 = (s32[128,8]{0,1:T(8,128)S(1)}, s32[128,8]{0,1:T(8,128)}, u32[]{:S(2)}) copy-start(s32[128,8]{0,1:T(8,128)} %param.12) | copy-start | bytes 12292
  3.3 19.7 %copy-start.4 = (s32[128,8]{0,1:T(8,128)S(1)}, s32[128,8]{0,1:T(8,128)}, u32[]{:S(2)}) copy-start(s32[128,8]{0,1:T(8,128)} %param.13) | copy-start | bytes 12292
  3.3 19.7 %copy-start.6 = (s32[128]{0:T(128)S(1)}, s32[128]{0:T(128)}, u32[]{:S(2)}) copy-start(s32[128]{0:T(128)} %param.11) | copy-start | bytes 1540
  6.4 36.6 %copy-start.2 = (bf16[4,2,256,256]{3,2,1,0:T(8,128)(2,1)S(1)}, bf16[4,2,256,256]{3,2,1,0:T(8,128)(2,1)}, u32[]{:S(2)}) copy-start(bf16[4,2,256,256]{3,2,1,0:T(8,128)(2,1)} %delta.1) | copy-start | bytes 3145732
  6.4 31.2 %all-to-all-start = ((bf16[64,9,2,128]{3,2,1,0:T(2,128)(2,1)}), bf16[64,9,2,128]{3,2,1,0:T(2,128)(2,1)S(1)}, u32[]{:S(2)}, u32[]{:S(2)}) async-start(bf16[64,9,2,128]{3,2,1,0:T(2,128)(2,1)} %bitcast.2), calls=%async_computation | async-start | bytes 589824 | tf_op jit(solution)/shard_map/all_to_all | solution.py:195
  38.5 9.9 %all-to-all-start.1 = ((f32[8,8,512]{2,1,0:T(8,128)}), f32[8,8,512]{2,1,0:T(8,128)S(1)}, u32[]{:S(2)}, u32[]{:S(2)}) async-start(f32[8,8,512]{2,1,0:T(8,128)} %phase_sum.1), calls=%async_computation.1 | async-start | bytes 262144 | tf_op jit(solution)/shard_map/all_to_all | solution.py:222

commit v2 on v1

--- a/solution.py
+++ b/solution.py
@@ -33,13 +33,13 @@
     return tables
 
 
-def solve_kernel(spot, grid, lattice, matrix, out, wide):
+def solve_kernel(grid, lattice, matrix, out, wide):
     kpoints, _, order, _ = matrix.shape
     own = order // 4
     chunk = out.shape[0] // own
     row = lax.broadcasted_iota(jnp.int32, (own, order), 0)
     col = lax.broadcasted_iota(jnp.int32, (own, order), 1)
-    pick = jnp.where(col == row * 4 + spot[0], 1.0, 0.0).astype(BF16)
+    pick = jnp.where(col == row * 4 + lax.axis_index("pair"), 1.0, 0.0).astype(BF16)
     first = [[dot(pick, matrix[k, part]) for part in range(2)] for k in range(kpoints)]
     now = [list(pair) for pair in first]
     for step in range(ITERS - 1):
@@ -67,15 +67,15 @@
                 wide[pl.ds(place, own, stride=chunk), :] = now[k][part][
                     :, half * LANES : (half + 1) * LANES
                 ]
-    vectors = lattice.shape[0]
+    vectors = lattice.shape[1]
     lane = lax.broadcasted_iota(jnp.int32, (8, LANES), 1)
     turn = jnp.zeros((8, LANES), jnp.int32)
     for r in range(vectors):
         for k in range(kpoints):
             m = (
-                grid[k, 0] * lattice[r, 0]
-                + grid[k, 1] * lattice[r, 1]
-                + grid[k, 2] * lattice[r, 2]
+                grid[k, 0] * lattice[0, r]
+                + grid[k, 1] * lattice[1, r]
+                + grid[k, 2] * lattice[2, r]
             ) & (KG - 1)
             here = ((lane // (4 * vectors)) == k) & ((lane & (vectors - 1)) == r)
             turn = jnp.where(here, m, turn)
@@ -110,57 +110,78 @@
     out[...] = jnp.broadcast_to(both[None], out.shape)
 
 
-def coupling_kernel(spot, delta, out):
+def product_kernel(scale, parts, delta, route, species, count, host, out, wide, sums):
+    vectors = parts.shape[1]
     kinds, _, order, _ = delta.shape
-    row = lax.broadcasted_iota(jnp.int32, (order, LANES), 0)
-    col = lax.broadcasted_iota(jnp.int32, (order, LANES), 1)
-    half = LANES // 2
-    left = ((col < half) & (row == spot[0] * half + col)).astype(F32).astype(BF16)
-    right = ((col >= half) & (row == spot[0] * half + col - half)).astype(F32).astype(BF16)
-    for s in range(kinds):
-        re, im = delta[s, 0], delta[s, 1]
-        out[:order, s * LANES : (s + 1) * LANES] = (dot(re, left) + dot(im, right)).astype(BF16)
-        out[order:, s * LANES : (s + 1) * LANES] = (dot(re, right) - dot(im, left)).astype(BF16)
-
-
-def product_kernel(scale, spot, parts, coupling, chosen, host, out, wide, sums):
-    vectors = parts.shape[1]
-    order = parts.shape[2] // 2
+    slots, owners = route.shape
+    pair, core = lax.axis_index("pair"), lax.axis_index("c")
     half = LANES // 2
     for q in range(4):
         sums[q * vectors : (q + 1) * vectors, :] = (parts[q] + parts[4 + q]) * scale
-    own = pl.multiple_of(spot[1] * (2 * vectors), 2 * vectors)
-    at = pl.multiple_of((spot[0] // 2) * LANES, LANES)
-    re = sums[pl.ds(own, 2 * vectors), pl.ds(at, LANES)]
-    im = sums[pl.ds(own, 2 * vectors), pl.ds(order + at, LANES)]
-    lane = lax.broadcasted_iota(jnp.int32, re.shape, 1)
-    odd = (spot[0] & 1) == 1
-    re = jnp.where(odd, pltpu.roll(re, half, 1), re)
-    im = jnp.where(odd, im, pltpu.roll(im, half, 1))
-    host[...] = jnp.where(lane < half, re, im)
-    product = dot(sums[...].astype(BF16), coupling[...])
-    kinds = coupling.shape[1] // LANES
-    table = jnp.concatenate(
-        [
-            jnp.concatenate(
-                [
-                    product[q * vectors : (q + 1) * vectors, s * LANES : (s + 1) * LANES]
-                    for q in range(4)
-                ],
-                axis=1,
-            )
-            for s in range(kinds)
-        ],
-        axis=0,
-    ).astype(BF16)
-    picked = dot(chosen[...], table)
-    for q in range(4):
-        wide[pl.ds(q, picked.shape[0], stride=4), :] = picked[:, q * LANES : (q + 1) * LANES]
+    odd = (pair & 1) == 1
+    lane = lax.broadcasted_iota(jnp.int32, (1, LANES), 1)
+
+    def window(re, im):
+        re = jnp.where(odd, pltpu.roll(re, half, 1), re)
+        im = jnp.where(odd, im, pltpu.roll(im, half, 1))
+        return jnp.where(lane < half, re, im)
+
+    own = pl.multiple_of(core * (2 * vectors), 2 * vectors)
+    at = pl.multiple_of((pair // 2) * LANES, LANES)
+    host[...] = window(
+        sums[pl.ds(own, 2 * vectors), pl.ds(at, LANES)],
+        sums[pl.ds(own, 2 * vectors), pl.ds(order + at, LANES)],
+    )
+    rows = 4 * vectors
+    left = jnp.concatenate([sums[:, :order], sums[:, order:]], axis=0).astype(BF16)
+    table = []
+    for s in range(kinds):
+        u = dot(left, delta[s, 0])
+        v = dot(left, delta[s, 1])
+        re = u[:rows] - v[rows:]
+        im = v[:rows] + u[rows:]
+        re = jnp.where(pair >= 2, re[:, LANES:], re[:, :LANES])
+        im = jnp.where(pair >= 2, im[:, LANES:], im[:, :LANES])
+        product = window(re, im)
+        table.append(
+            jnp.concatenate([product[q * vectors : (q + 1) * vectors] for q in range(4)], axis=1)
+        )
+    table = jnp.concatenate(table, axis=0).astype(BF16)
+    alive = lax.broadcasted_iota(jnp.int32, (slots, owners), 0) < count[...]
+    combo = jnp.where(alive, species[...] * vectors + route[...], kinds * vectors)
+    combo = jnp.transpose(combo.astype(F32)).astype(BF16)
+    chips = owners // 2
+    row = lax.broadcasted_iota(jnp.int32, (chips, owners), 0)
+    col = lax.broadcasted_iota(jnp.int32, (chips, owners), 1)
+    combo = dot(jnp.where(col == row * 2 + core, 1.0, 0.0).astype(BF16), combo)
+    kind = lax.broadcasted_iota(jnp.int32, (chips, kinds * vectors), 1).astype(F32)
+    chosen = [
+        jnp.where(jnp.broadcast_to(combo[:, t : t + 1], kind.shape) == kind, 1.0, 0.0)
+        for t in range(slots)
+    ]
+    chosen = jnp.concatenate(chosen, axis=0).astype(BF16)
+    picked = dot(chosen, table)
+    for t in range(slots):
+        for q in range(4):
+            wide[pl.ds(t * 4 + q, chips, stride=4 * slots), :] = picked[
+                t * chips : (t + 1) * chips, q * LANES : (q + 1) * LANES
+            ]
     out[...] = wide[...].astype(BF16)
+
+
+def place_kernel(got, out, sems):
+    copies = [
+        pltpu.make_async_copy(got.at[:, t], out.at[t], sems.at[t]) for t in range(out.shape[0])
+    ]
+    for copy in copies:
+        copy.start()
+    for copy in copies:
+        copy.wait()
 
 
 VMEM = pl.BlockSpec(memory_space=pltpu.VMEM)
 SMEM = pl.BlockSpec(memory_space=pltpu.SMEM)
+HBM = pl.BlockSpec(memory_space=pltpu.HBM)
 
 
 def params():
@@ -170,14 +191,10 @@
 def per_device(kkr_matrix, kpoint_grid, lattice, delta_t, pair_count, pair_route, species):
     chips = lax.axis_size(CHIPS)
     cores = lax.axis_size(CORES)
-    pair = lax.axis_index("pair")
-    core = lax.axis_index("c")
-    spot = jnp.stack([pair, core]).astype(jnp.int32)
     order = kkr_matrix.shape[2]
     kpoints = kkr_matrix.shape[0]
     vectors = lattice.shape[0]
     slots = pair_route.shape[1]
-    kinds = delta_t.shape[0]
     scale = math.sqrt(order / (kpoints * chips * lax.axis_size("c")))
     chunk = 4 * kpoints + 2
     length = chips * chunk
@@ -185,30 +202,14 @@
     outgoing = pl.pallas_call(
         solve_kernel,
         out_shape=jax.ShapeDtypeStruct((length, LANES), BF16),
-        in_specs=[SMEM, SMEM, SMEM, VMEM],
+        in_specs=[SMEM, SMEM, VMEM],
         out_specs=VMEM,
         scratch_shapes=[pltpu.VMEM((length, LANES), F32)],
         compiler_params=params(),
         name="solve",
-    )(spot, kpoint_grid, lattice, kkr_matrix)
+    )(kpoint_grid, lattice.T, kkr_matrix)
     outgoing = outgoing.reshape(chips, chunk // 2, 2, LANES)
     arrived = lax.all_to_all(outgoing, CHIPS, split_axis=0, concat_axis=0, tiled=True)
-
-    coupling = pl.pallas_call(
-        coupling_kernel,
-        out_shape=jax.ShapeDtypeStruct((2 * order, kinds * LANES), BF16),
-        in_specs=[SMEM, VMEM],
-        out_specs=VMEM,
-        compiler_params=params(),
-        cost_estimate=pl.CostEstimate(
-            flops=16 * kinds * order * order * LANES, bytes_accessed=2 << 20, transcendentals=0
-        ),
-        name="coupling",
-    )(spot, delta_t)
-    alive = jnp.arange(slots)[None, :] < pair_count[:, None]
-    combo = jnp.where(alive, species * vectors + pair_route, -1)
-    combo = lax.dynamic_index_in_dim(combo.reshape(chips, 2, slots), core, 1, keepdims=False)
-    chosen = (combo.reshape(-1, 1) == jnp.arange(kinds * vectors)[None, :]).astype(BF16)
 
     parts = pl.pallas_call(
         functools.partial(phase_kernel, kpoints, vectors),
@@ -227,7 +228,7 @@
             jax.ShapeDtypeStruct((2 * vectors, LANES), F32),
             jax.ShapeDtypeStruct((chips * slots * 4, LANES), BF16),
         ),
-        in_specs=[SMEM, VMEM, VMEM, VMEM],
+        in_specs=[VMEM, VMEM, VMEM, VMEM, VMEM],
         out_specs=(VMEM, VMEM),
         scratch_shapes=[
             pltpu.VMEM((chips * slots * 4, LANES), F32),
@@ -235,10 +236,18 @@
         ],
         compiler_params=params(),
         name="product",
-    )(spot, parts, coupling, chosen)
+    )(parts, delta_t, pair_route.T, species.T, pair_count[None])
     sent = sent.reshape(chips, slots * 4, LANES)
     got = lax.all_to_all(sent, CHIPS, split_axis=0, concat_axis=0, tiled=True)
-    cluster = got.reshape(chips, slots, 4, LANES).transpose(1, 0, 2, 3)
+    cluster = pl.pallas_call(
+        place_kernel,
+        out_shape=jax.ShapeDtypeStruct((slots, chips, 4, LANES), BF16),
+        in_specs=[VMEM],
+        out_specs=HBM,
+        scratch_shapes=[pltpu.SemaphoreType.DMA((slots,))],
+        compiler_params=params(),
+        name="place",
+    )(got.reshape(chips, slots, 4, LANES))
     return (host_rows, cluster.reshape(slots, order, LANES))
 
 

time: 75.9 us -> 74.4 us (0.980)
  blocking collectives: 24.6 us -> 65.1 us
  starting transfers between devices: 20.9 us -> 0 us
  waiting for transfers between devices: 18.4 us -> 0 us
  Pallas kernels: 6.82 us -> 4.98 us
    all_to_all x0 -> x2, blocking collectives: none -> 40.5 us  [the longest x1 30.9 us: per_device(): lax.all_to_all(outgoing, CHIPS, split_axis=0, concat_axis=0, tiled=True)]
    all_to_all x2 -> x0, starting transfers between devices: 20.9 us -> none  [the longest x1 16.6 us: per_device(): lax.all_to_all(outgoing, CHIPS, split_axis=0, concat_axis=0, tiled=True)]
    all_to_all x2 -> x0, waiting for transfers between devices: 18.4 us -> none  [the longest x1 14.3 us: per_device(): lax.all_to_all(outgoing, CHIPS, split_axis=0, concat_axis=0, tiled=True)]
    reshape x1 -> x0, local copies, waits for them, and re-layouts: 1 us -> none  [per_device(): cluster = got.reshape(chips, slots, 4, LANES).transpose(1, 0, 2, 3)]
    unnamed x15 -> x14, local copies, waits for them, and re-layouts: 2.6 us -> 3.27 us
  transfers between devices with their start and end apart: 2 -> 0, of which waited for: 2 -> 0; matrix products, arithmetic and copies ran while one was open for 1% -> 0% of each run, Pallas kernels for 2% -> 0%
where the time goes in v2:
time: 74.4 us; the launch traced here: 74 us
  blocking collectives  65.1 us (87%)
  Pallas kernels  4.98 us (7%)
  local copies, waits for them, and re-layouts  3.27 us (4%)
    all_to_all x1, blocking collectives, per_device(): lax.all_to_all(outgoing, CHIPS, split_axis=0, concat_axis=0, tiled=True)  30.9 us
    all_to_all x1, blocking collectives, per_device(): got = lax.all_to_all(sent, CHIPS, split_axis=0, concat_axis=0, tiled=True)  24.6 us
    all_to_all x1, blocking collectives, per_device(): lax.all_to_all(parts, CORES, split_axis=0, concat_axis=0, tiled=True)  9.65 us
    unnamed x14, local copies, waits for them, and re-layouts  3.27 us
    pallas_call x1, Pallas kernels, per_device(): pl.pallas_call(solve_kernel, out_shape=jax.ShapeDtypeStruct((length, LANE...  2.37 us
    pallas_call x1, Pallas kernels, per_device(): pl.pallas_call(functools.partial(product_kernel, scale), out_shape=(jax.S...  1.49 us

profile of v2, /device:TPU:16, one launch (start us, length us, event | category | flops | bytes accessed | tf_op | source)
XLA Modules:
  0.0 74.0 jit_solution(3265966068759076094)
XLA Ops:
  0.6 0.0 copy-start
  0.6 1.2 %copy-done = bf16[4,2,256,256]{3,2,1,0:T(8,128)(2,1)S(1)} copy-done((bf16[4,2,256,256]{3,2,1,0:T(8,128)(2,1)S(1)}, bf16[4,2,256,256]{3,2,1,0:T(8,128)(2,1)}, u32[]{:S(2)}) %copy-start) | copy-done | bytes 1048600
  1.9 0.0 copy-start.4
  1.9 0.7 copy-done.4
  2.5 0.0 copy-start.5
  2.5 0.7 copy-done.5
  3.2 0.0 copy-start.1
  3.2 2.4 %solve.1 = bf16[1152,128]{1,0:T(8,128)(2,1)S(1)} custom-call(s32[4,3]{1,0:T(4,128)S(1)} %copy-done.4, s32[3,8]{1,0:T(4,128)S(1)} %bitcast.15, bf16[4,2,256,256]{3,2,1,0:T(8,128)(2,1)S(1)} %copy-done), custom_call_target="tpu_custom_call" | custom-call | tf_op jit(solution)/shard_map/solve/pallas_call | solution.py:202
  5.6 30.9 %all_to_all.15 = bf16[64,9,2,128]{3,2,1,0:T(2,128)(2,1)S(1)} all-to-all(bf16[64,9,2,128]{3,2,1,0:T(2,128)(2,1)S(1)} %bitcast.11), channel_id=1, replica_groups=mesh['y'=8,'z'=8,'c'=2,'pair'=4] {'y','z'}, dimensions={0} | all-to-all | bytes 589824 | tf_op jit(solution)/shard_map/all_to_all | solution.py:212
  36.5 0.3 phase_sum.1
  36.8 0.0 copy-start.3
  36.8 9.7 %all_to_all.16.parts = f32[8,8,512]{2,1,0:T(8,128)S(1)} all-to-all(f32[8,8,512]{2,1,0:T(8,128)S(1)} %phase_sum.1), channel_id=1, replica_groups=mesh['y'=8,'z'=8,'c'=2,'pair'=4] {'c','pair'}, dimensions={0} | all-to-all | bytes 262144 | tf_op jit(solution)/shard_map/all_to_all | solution.py:223
  46.4 0.0 copy-start.2
  46.4 0.0 copy-start.6
  46.4 0.0 copy-done.1
  46.4 0.0 copy-done.3
  46.5 0.7 copy-done.2
  47.1 0.0 copy-done.6
  47.1 1.5 %product.1 = (f32[16,128]{1,0:T(8,128)}, bf16[2048,128]{1,0:T(8,128)(2,1)S(1)}) custom-call(f32[8,8,512]{2,1,0:T(8,128)S(1)} %all_to_all.16.parts, bf16[4,2,256,256]{3,2,1,0:T(8,128)(2,1)S(1)} %copy-done.1, s32[8,128]{1,0:T(8,128)S(1)} %bitcast.13, s32[8,128]{1,0:T(8,128)S(1)} %bitcast.14, s32[1,128]{1,0:T(1,128)S(1)} %bitcast.16), custom_call_target="tpu_custom_call" | custom-call | tf_op jit(solution)/shard_map/product/pallas_call | solution.py:225
  48.6 24.6 %all_to_all.17 = bf16[64,32,128]{2,1,0:T(8,128)(2,1)S(1)} all-to-all(bf16[64,32,128]{2,1,0:T(8,128)(2,1)S(1)} %bitcast.12), channel_id=1, replica_groups=mesh['y'=8,'z'=8,'c'=2,'pair'=4] {'y','z'}, dimensions={0} | all-to-all | bytes 1048576 | tf_op jit(solution)/shard_map/all_to_all | solution.py:241
  73.2 0.8 %place.1 = bf16[8,64,4,128]{3,2,1,0:T(4,128)(2,1)} custom-call(bf16[64,8,4,128]{3,2,1,0:T(4,128)(2,1)S(1)} %bitcast.9), custom_call_target="tpu_custom_call" | custom-call | tf_op jit(solution)/shard_map/place/pallas_call | solution.py:242
Async XLA Ops:
  0.6 1.2 %copy-start = (bf16[4,2,256,256]{3,2,1,0:T(8,128)(2,1)S(1)}, bf16[4,2,256,256]{3,2,1,0:T(8,128)(2,1)}, u32[]{:S(2)}) copy-start(bf16[4,2,256,256]{3,2,1,0:T(8,128)(2,1)} %matrix.1) | copy-start | bytes 3145732
  1.9 0.7 copy-start.4
  2.5 0.7 copy-start.5
  3.2 43.2 %copy-start.1 = (bf16[4,2,256,256]{3,2,1,0:T(8,128)(2,1)S(1)}, bf16[4,2,256,256]{3,2,1,0:T(8,128)(2,1)}, u32[]{:S(2)}) copy-start(bf16[4,2,256,256]{3,2,1,0:T(8,128)(2,1)} %delta.1) | copy-start | bytes 3145732
  36.8 9.7 %copy-start.3 = (s32[128,8]{0,1:T(8,128)S(1)}, s32[128,8]{0,1:T(8,128)}, u32[]{:S(2)}) copy-start(s32[128,8]{0,1:T(8,128)} %param.13) | copy-start | bytes 12292
  46.4 0.7 copy-start.2
  46.4 0.7 copy-start.6

commit v3 on v2

--- a/solution.py
+++ b/solution.py
@@ -33,14 +33,29 @@
     return tables
 
 
-def solve_kernel(grid, lattice, matrix, out, wide):
+def fetch(places, sems):
+    copies = [
+        pltpu.make_async_copy(start, end, sems.at[i]) for i, (start, end) in enumerate(places)
+    ]
+    for copy in copies:
+        copy.start()
+    return copies
+
+
+def solve_kernel(grid_in, lattice_in, matrix_in, out, grid, lattice, matrix, wide, sems):
     kpoints, _, order, _ = matrix.shape
     own = order // 4
     chunk = out.shape[0] // own
+    places = [(matrix_in.at[k, i], matrix.at[k, i]) for k in range(kpoints) for i in range(2)]
+    copies = fetch(places + [(grid_in, grid), (lattice_in, lattice)], sems)
     row = lax.broadcasted_iota(jnp.int32, (own, order), 0)
     col = lax.broadcasted_iota(jnp.int32, (own, order), 1)
     pick = jnp.where(col == row * 4 + lax.axis_index("pair"), 1.0, 0.0).astype(BF16)
-    first = [[dot(pick, matrix[k, part]) for part in range(2)] for k in range(kpoints)]
+    first = []
+    for k in range(kpoints):
+        copies[2 * k].wait()
+        copies[2 * k + 1].wait()
+        first.append([dot(pick, matrix[k, part]) for part in range(2)])
     now = [list(pair) for pair in first]
     for step in range(ITERS - 1):
         for k in range(kpoints):
@@ -67,6 +82,8 @@
                 wide[pl.ds(place, own, stride=chunk), :] = now[k][part][
                     :, half * LANES : (half + 1) * LANES
                 ]
+    copies[-2].wait()
+    copies[-1].wait()
     vectors = lattice.shape[1]
     lane = lax.broadcasted_iota(jnp.int32, (8, LANES), 1)
     turn = jnp.zeros((8, LANES), jnp.int32)
@@ -110,10 +127,14 @@
     out[...] = jnp.broadcast_to(both[None], out.shape)
 
 
-def product_kernel(scale, parts, delta, route, species, count, host, out, wide, sums):
+def product_kernel(
+    scale, parts, delta, route_in, species_in, count_in, host, out, wide, sums, *scratch
+):
     vectors = parts.shape[1]
     kinds, _, order, _ = delta.shape
+    route, species, count, sems = scratch
     slots, owners = route.shape
+    copies = fetch([(route_in, route), (species_in, species), (count_in, count)], sems)
     pair, core = lax.axis_index("pair"), lax.axis_index("c")
     half = LANES // 2
     for q in range(4):
@@ -147,6 +168,8 @@
             jnp.concatenate([product[q * vectors : (q + 1) * vectors] for q in range(4)], axis=1)
         )
     table = jnp.concatenate(table, axis=0).astype(BF16)
+    for copy in copies:
+        copy.wait()
     alive = lax.broadcasted_iota(jnp.int32, (slots, owners), 0) < count[...]
     combo = jnp.where(alive, species[...] * vectors + route[...], kinds * vectors)
     combo = jnp.transpose(combo.astype(F32)).astype(BF16)
@@ -184,6 +207,10 @@
 HBM = pl.BlockSpec(memory_space=pltpu.HBM)
 
 
+def in_hbm(x):
+    return pltpu.with_memory_space_constraint(x, pltpu.HBM)
+
+
 def params():
     return pltpu.CompilerParams(vmem_limit_bytes=32 * 1024 * 1024)
 
@@ -202,12 +229,18 @@
     outgoing = pl.pallas_call(
         solve_kernel,
         out_shape=jax.ShapeDtypeStruct((length, LANES), BF16),
-        in_specs=[SMEM, SMEM, VMEM],
+        in_specs=[HBM, HBM, HBM],
         out_specs=VMEM,
-        scratch_shapes=[pltpu.VMEM((length, LANES), F32)],
+        scratch_shapes=[
+            pltpu.SMEM((kpoints, 3), jnp.int32),
+            pltpu.SMEM((3, vectors), jnp.int32),
+            pltpu.VMEM(kkr_matrix.shape, BF16),
+            pltpu.VMEM((length, LANES), F32),
+            pltpu.SemaphoreType.DMA((2 * kpoints + 2,)),
+        ],
         compiler_params=params(),
         name="solve",
-    )(kpoint_grid, lattice.T, kkr_matrix)
+    )(in_hbm(kpoint_grid), in_hbm(lattice.T), in_hbm(kkr_matrix))
     outgoing = outgoing.reshape(chips, chunk // 2, 2, LANES)
     arrived = lax.all_to_all(outgoing, CHIPS, split_axis=0, concat_axis=0, tiled=True)
 
@@ -228,15 +261,19 @@
             jax.ShapeDtypeStruct((2 * vectors, LANES), F32),
             jax.ShapeDtypeStruct((chips * slots * 4, LANES), BF16),
         ),
-        in_specs=[VMEM, VMEM, VMEM, VMEM, VMEM],
+        in_specs=[VMEM, VMEM, HBM, HBM, HBM],
         out_specs=(VMEM, VMEM),
         scratch_shapes=[
             pltpu.VMEM((chips * slots * 4, LANES), F32),
             pltpu.VMEM((4 * vectors, 2 * order), F32),
+            pltpu.VMEM(pair_route.T.shape, jnp.int32),
+            pltpu.VMEM(species.T.shape, jnp.int32),
+            pltpu.VMEM((1,) + pair_count.shape, jnp.int32),
+            pltpu.SemaphoreType.DMA((3,)),
         ],
         compiler_params=params(),
         name="product",
-    )(parts, delta_t, pair_route.T, species.T, pair_count[None])
+    )(parts, delta_t, in_hbm(pair_route.T), in_hbm(species.T), in_hbm(pair_count[None]))
     sent = sent.reshape(chips, slots * 4, LANES)
     got = lax.all_to_all(sent, CHIPS, split_axis=0, concat_axis=0, tiled=True)
     cluster = pl.pallas_call(

time: 74.4 us -> 72.5 us (0.974)
  local copies, waits for them, and re-layouts: 3.27 us -> 0.01 us
  Pallas kernels: 4.98 us -> 6.49 us
    unnamed x14 -> x2, local copies, waits for them, and re-layouts: 3.27 us -> 0.01 us
    pallas_call x1, Pallas kernels: 2.37 us -> 3.38 us  [per_device(): pl.pallas_call(solve_kernel, out_shape=jax.ShapeDtypeStruct((length, LANE...]
where the time goes in v3:
time: 72.5 us; the launch traced here: 72.3 us
  blocking collectives  65.1 us (90%)
  Pallas kernels  6.49 us (9%)
    all_to_all x1, blocking collectives, per_device(): lax.all_to_all(outgoing, CHIPS, split_axis=0, concat_axis=0, tiled=True)  30.9 us
    all_to_all x1, blocking collectives, per_device(): got = lax.all_to_all(sent, CHIPS, split_axis=0, concat_axis=0, tiled=True)  24.6 us
    all_to_all x1, blocking collectives, per_device(): lax.all_to_all(parts, CORES, split_axis=0, concat_axis=0, tiled=True)  9.65 us
    pallas_call x1, Pallas kernels, per_device(): pl.pallas_call(solve_kernel, out_shape=jax.ShapeDtypeStruct((length, LANE...  3.38 us
    pallas_call x1, Pallas kernels, per_device(): pl.pallas_call(functools.partial(product_kernel, scale), out_shape=(jax.S...  1.99 us

profile of v3, /device:TPU:16, one launch (start us, length us, event | category | flops | bytes accessed | tf_op | source)
XLA Modules:
  0.0 72.3 jit_solution(11133950029046866761)
XLA Ops:
  0.6 0.0 copy-start
  0.6 3.4 %solve.1 = bf16[1152,128]{1,0:T(8,128)(2,1)S(1)} custom-call(s32[4,3]{1,0:T(4,128)} %grid_in.1, s32[3,8]{1,0:T(4,128)} %bitcast.16, bf16[4,2,256,256]{3,2,1,0:T(8,128)(2,1)} %matrix_in.1), custom_call_target="tpu_custom_call" | custom-call | tf_op jit(solution)/shard_map/solve/pallas_call | solution.py:229
  4.0 30.9 %all_to_all.15 = bf16[64,9,2,128]{3,2,1,0:T(2,128)(2,1)S(1)} all-to-all(bf16[64,9,2,128]{3,2,1,0:T(2,128)(2,1)S(1)} %bitcast.11), channel_id=1, replica_groups=mesh['y'=8,'z'=8,'c'=2,'pair'=4] {'y','z'}, dimensions={0} | all-to-all | bytes 589824 | tf_op jit(solution)/shard_map/all_to_all | solution.py:245
  34.9 0.3 phase_sum.1
  35.2 9.7 %all_to_all.16.parts = f32[8,8,512]{2,1,0:T(8,128)S(1)} all-to-all(f32[8,8,512]{2,1,0:T(8,128)S(1)} %phase_sum.1), channel_id=1, replica_groups=mesh['y'=8,'z'=8,'c'=2,'pair'=4] {'c','pair'}, dimensions={0} | all-to-all | bytes 262144 | tf_op jit(solution)/shard_map/all_to_all | solution.py:256
  44.9 0.0 copy-done
  44.9 2.0 %product.1 = (f32[16,128]{1,0:T(8,128)}, bf16[2048,128]{1,0:T(8,128)(2,1)S(1)}) custom-call(f32[8,8,512]{2,1,0:T(8,128)S(1)} %all_to_all.16.parts, bf16[4,2,256,256]{3,2,1,0:T(8,128)(2,1)S(1)} %copy-done, s32[8,128]{1,0:T(8,128)} %bitcast.14, s32[8,128]{1,0:T(8,128)} %bitcast.15, s32[1,128]{1,0:T(1,128)} %bitcast.17), custom_call_target="tpu_custom_call" | custom-call | tf_op jit(solution)/shard_map/product/pallas_call | solution.py:258
  46.9 24.6 %all_to_all.17 = bf16[64,32,128]{2,1,0:T(8,128)(2,1)S(1)} all-to-all(bf16[64,32,128]{2,1,0:T(8,128)(2,1)S(1)} %bitcast.12), channel_id=1, replica_groups=mesh['y'=8,'z'=8,'c'=2,'pair'=4] {'y','z'}, dimensions={0} | all-to-all | bytes 1048576 | tf_op jit(solution)/shard_map/all_to_all | solution.py:278
  71.4 0.8 %place.1 = bf16[8,64,4,128]{3,2,1,0:T(4,128)(2,1)} custom-call(bf16[64,8,4,128]{3,2,1,0:T(4,128)(2,1)S(1)} %bitcast.9), custom_call_target="tpu_custom_call" | custom-call | tf_op jit(solution)/shard_map/place/pallas_call | solution.py:279
Async XLA Ops:
  0.6 44.2 %copy-start = (bf16[4,2,256,256]{3,2,1,0:T(8,128)(2,1)S(1)}, bf16[4,2,256,256]{3,2,1,0:T(8,128)(2,1)}, u32[]{:S(2)}) copy-start(bf16[4,2,256,256]{3,2,1,0:T(8,128)(2,1)} %delta.1) | copy-start | bytes 3145732

commit v4 on v3

--- a/solution.py
+++ b/solution.py
@@ -42,19 +42,47 @@
     return copies
 
 
-def solve_kernel(grid_in, lattice_in, matrix_in, out, grid, lattice, matrix, wide, sems):
+def solve_kernel(
+    kinds, grid_in, lattice_in, matrix_in, route_in, species_in, count_in, out, combo, *scratch
+):
+    grid, lattice, matrix, route, species, count, wide, sems = scratch
     kpoints, _, order, _ = matrix.shape
     own = order // 4
     chunk = out.shape[0] // own
     places = [(matrix_in.at[k, i], matrix.at[k, i]) for k in range(kpoints) for i in range(2)]
-    copies = fetch(places + [(grid_in, grid), (lattice_in, lattice)], sems)
+    places = [(grid_in, grid), (lattice_in, lattice)] + places
+    places += [(route_in, route), (species_in, species), (count_in, count)]
+    copies = fetch(places, sems)
+    small, large, late = copies[:2], copies[2:-3], copies[-3:]
+    for copy in small:
+        copy.wait()
+    vectors = lattice.shape[1]
+    lane = lax.broadcasted_iota(jnp.int32, (8, LANES), 1)
+    turn = jnp.zeros((8, LANES), jnp.int32)
+    for r in range(vectors):
+        for k in range(kpoints):
+            m = (
+                grid[k, 0] * lattice[0, r]
+                + grid[k, 1] * lattice[1, r]
+                + grid[k, 2] * lattice[2, r]
+            ) & (KG - 1)
+            here = ((lane // (4 * vectors)) == k) & ((lane & (vectors - 1)) == r)
+            turn = jnp.where(here, m, turn)
+    kind = (lane // vectors) & 3
+    phase = jnp.zeros((8, LANES), F32)
+    for which, table in enumerate(turn_tables()):
+        for m in range(KG):
+            phase = jnp.where((kind == which) & (turn == m), float(table[m]), phase)
+    phase = jnp.broadcast_to(phase[:1], (own, LANES))
+    wide[pl.ds(chunk - 2, own, stride=chunk), :] = phase
+    wide[pl.ds(chunk - 1, own, stride=chunk), :] = jnp.zeros((own, LANES), F32)
     row = lax.broadcasted_iota(jnp.int32, (own, order), 0)
     col = lax.broadcasted_iota(jnp.int32, (own, order), 1)
     pick = jnp.where(col == row * 4 + lax.axis_index("pair"), 1.0, 0.0).astype(BF16)
     first = []
     for k in range(kpoints):
-        copies[2 * k].wait()
-        copies[2 * k + 1].wait()
+        large[2 * k].wait()
+        large[2 * k + 1].wait()
         first.append([dot(pick, matrix[k, part]) for part in range(2)])
     now = [list(pair) for pair in first]
     for step in range(ITERS - 1):
@@ -82,28 +110,10 @@
                 wide[pl.ds(place, own, stride=chunk), :] = now[k][part][
                     :, half * LANES : (half + 1) * LANES
                 ]
-    copies[-2].wait()
-    copies[-1].wait()
-    vectors = lattice.shape[1]
-    lane = lax.broadcasted_iota(jnp.int32, (8, LANES), 1)
-    turn = jnp.zeros((8, LANES), jnp.int32)
-    for r in range(vectors):
-        for k in range(kpoints):
-            m = (
-                grid[k, 0] * lattice[0, r]
-                + grid[k, 1] * lattice[1, r]
-                + grid[k, 2] * lattice[2, r]
-            ) & (KG - 1)
-            here = ((lane // (4 * vectors)) == k) & ((lane & (vectors - 1)) == r)
-            turn = jnp.where(here, m, turn)
-    kind = (lane // vectors) & 3
-    phase = jnp.zeros((8, LANES), F32)
-    for which, table in enumerate(turn_tables()):
-        for m in range(KG):
-            phase = jnp.where((kind == which) & (turn == m), float(table[m]), phase)
-    phase = jnp.broadcast_to(phase[:1], (own, LANES))
-    wide[pl.ds(chunk - 2, own, stride=chunk), :] = phase
-    wide[pl.ds(chunk - 1, own, stride=chunk), :] = jnp.zeros((own, LANES), F32)
+    for copy in late:
+        copy.wait()
+    alive = lax.broadcasted_iota(jnp.int32, combo.shape, 0) < count[...]
+    combo[...] = jnp.where(alive, species[...] * vectors + route[...], kinds * vectors)
     out[...] = wide[...].astype(BF16)
 
 
@@ -127,14 +137,10 @@
     out[...] = jnp.broadcast_to(both[None], out.shape)
 
 
-def product_kernel(
-    scale, parts, delta, route_in, species_in, count_in, host, out, wide, sums, *scratch
-):
+def product_kernel(scale, parts, delta, combo, host, out, wide, sums):
     vectors = parts.shape[1]
     kinds, _, order, _ = delta.shape
-    route, species, count, sems = scratch
-    slots, owners = route.shape
-    copies = fetch([(route_in, route), (species_in, species), (count_in, count)], sems)
+    slots, owners = combo.shape
     pair, core = lax.axis_index("pair"), lax.axis_index("c")
     half = LANES // 2
     for q in range(4):
@@ -168,11 +174,7 @@
             jnp.concatenate([product[q * vectors : (q + 1) * vectors] for q in range(4)], axis=1)
         )
     table = jnp.concatenate(table, axis=0).astype(BF16)
-    for copy in copies:
-        copy.wait()
-    alive = lax.broadcasted_iota(jnp.int32, (slots, owners), 0) < count[...]
-    combo = jnp.where(alive, species[...] * vectors + route[...], kinds * vectors)
-    combo = jnp.transpose(combo.astype(F32)).astype(BF16)
+    combo = jnp.transpose(combo[...].astype(F32)).astype(BF16)
     chips = owners // 2
     row = lax.broadcasted_iota(jnp.int32, (chips, owners), 0)
     col = lax.broadcasted_iota(jnp.int32, (chips, owners), 1)
@@ -193,12 +195,15 @@
 
 
 def place_kernel(got, out, sems):
-    copies = [
-        pltpu.make_async_copy(got.at[:, t], out.at[t], sems.at[t]) for t in range(out.shape[0])
+    slots, chips = out.shape[:2]
+    cut = sems.shape[0] // slots
+    size = chips // cut
+    places = [
+        (got.at[i * size : (i + 1) * size, t], out.at[t, i * size : (i + 1) * size])
+        for t in range(slots)
+        for i in range(cut)
     ]
-    for copy in copies:
-        copy.start()
-    for copy in copies:
+    for copy in fetch(places, sems):
         copy.wait()
 
 
@@ -222,25 +227,33 @@
     kpoints = kkr_matrix.shape[0]
     vectors = lattice.shape[0]
     slots = pair_route.shape[1]
+    kinds = delta_t.shape[0]
     scale = math.sqrt(order / (kpoints * chips * lax.axis_size("c")))
     chunk = 4 * kpoints + 2
     length = chips * chunk
 
-    outgoing = pl.pallas_call(
-        solve_kernel,
-        out_shape=jax.ShapeDtypeStruct((length, LANES), BF16),
-        in_specs=[HBM, HBM, HBM],
-        out_specs=VMEM,
+    route, kind, count = pair_route.T, species.T, pair_count[None]
+    outgoing, combo = pl.pallas_call(
+        functools.partial(solve_kernel, kinds),
+        out_shape=(
+            jax.ShapeDtypeStruct((length, LANES), BF16),
+            jax.ShapeDtypeStruct(route.shape, jnp.int32),
+        ),
+        in_specs=[HBM] * 6,
+        out_specs=(VMEM, VMEM),
         scratch_shapes=[
             pltpu.SMEM((kpoints, 3), jnp.int32),
             pltpu.SMEM((3, vectors), jnp.int32),
             pltpu.VMEM(kkr_matrix.shape, BF16),
+            pltpu.VMEM(route.shape, jnp.int32),
+            pltpu.VMEM(kind.shape, jnp.int32),
+            pltpu.VMEM(count.shape, jnp.int32),
             pltpu.VMEM((length, LANES), F32),
-            pltpu.SemaphoreType.DMA((2 * kpoints + 2,)),
+            pltpu.SemaphoreType.DMA((2 * kpoints + 5,)),
         ],
         compiler_params=params(),
         name="solve",
-    )(in_hbm(kpoint_grid), in_hbm(lattice.T), in_hbm(kkr_matrix))
+    )(*map(in_hbm, (kpoint_grid, lattice.T, kkr_matrix, route, kind, count)))
     outgoing = outgoing.reshape(chips, chunk // 2, 2, LANES)
     arrived = lax.all_to_all(outgoing, CHIPS, split_axis=0, concat_axis=0, tiled=True)
 
@@ -261,19 +274,15 @@
             jax.ShapeDtypeStruct((2 * vectors, LANES), F32),
             jax.ShapeDtypeStruct((chips * slots * 4, LANES), BF16),
         ),
-        in_specs=[VMEM, VMEM, HBM, HBM, HBM],
+        in_specs=[VMEM, VMEM, VMEM],
         out_specs=(VMEM, VMEM),
         scratch_shapes=[
             pltpu.VMEM((chips * slots * 4, LANES), F32),
             pltpu.VMEM((4 * vectors, 2 * order), F32),
-            pltpu.VMEM(pair_route.T.shape, jnp.int32),
-            pltpu.VMEM(species.T.shape, jnp.int32),
-            pltpu.VMEM((1,) + pair_count.shape, jnp.int32),
-            pltpu.SemaphoreType.DMA((3,)),
         ],
         compiler_params=params(),
         name="product",
-    )(parts, delta_t, in_hbm(pair_route.T), in_hbm(species.T), in_hbm(pair_count[None]))
+    )(parts, delta_t, combo)
     sent = sent.reshape(chips, slots * 4, LANES)
     got = lax.all_to_all(sent, CHIPS, split_axis=0, concat_axis=0, tiled=True)
     cluster = pl.pallas_call(
@@ -281,7 +290,7 @@
         out_shape=jax.ShapeDtypeStruct((slots, chips, 4, LANES), BF16),
         in_specs=[VMEM],
         out_specs=HBM,
-        scratch_shapes=[pltpu.SemaphoreType.DMA((slots,))],
+        scratch_shapes=[pltpu.SemaphoreType.DMA((4 * slots,))],
         compiler_params=params(),
         name="place",
     )(got.reshape(chips, slots, 4, LANES))

time: 72.5 us -> 72.1 us (level)
  no operation moved by 1% of the time
where the time goes in v4:
time: 72.1 us; the launch traced here: 71.9 us
  blocking collectives  65.1 us (90%)
  Pallas kernels  6.07 us (8%)
    all_to_all x1, blocking collectives, per_device(): lax.all_to_all(outgoing, CHIPS, split_axis=0, concat_axis=0, tiled=True)  30.9 us
    all_to_all x1, blocking collectives, per_device(): got = lax.all_to_all(sent, CHIPS, split_axis=0, concat_axis=0, tiled=True)  24.6 us
    all_to_all x1, blocking collectives, per_device(): lax.all_to_all(parts, CORES, split_axis=0, concat_axis=0, tiled=True)  9.66 us
    pallas_call x1, Pallas kernels, per_device(): pl.pallas_call(functools.partial(solve_kernel, kinds), out_shape=(jax.Sha...  3.26 us
    pallas_call x1, Pallas kernels, per_device(): pl.pallas_call(functools.partial(product_kernel, scale), out_shape=(jax.S...  1.49 us

profile of v4, /device:TPU:16, one launch (start us, length us, event | category | flops | bytes accessed | tf_op | source)
XLA Modules:
  0.0 71.9 jit_solution(3743057199184827533)
XLA Ops:
  0.6 0.0 copy-start
  0.6 3.3 %solve.1 = (bf16[1152,128]{1,0:T(8,128)(2,1)S(1)}, s32[8,128]{1,0:T(8,128)S(1)}) custom-call(s32[4,3]{1,0:T(4,128)} %grid_in.1, s32[3,8]{1,0:T(4,128)} %bitcast.16, bf16[4,2,256,256]{3,2,1,0:T(8,128)(2,1)} %matrix_in.1, s32[8,128]{1,0:T(8,128)} %bitcast.14, s32[8,128]{1,0:T(8,128)} %bitcast.15, s32[1,128]{1,0:T(1,128)} %bitcast.17), custom_call_target="tpu_custom_call" | custom-call | tf_op jit(solution)/shard_map/solve/pallas_call | solution.py:236
  3.9 30.9 %all_to_all.15 = bf16[64,9,2,128]{3,2,1,0:T(2,128)(2,1)S(1)} all-to-all(bf16[64,9,2,128]{3,2,1,0:T(2,128)(2,1)S(1)} %bitcast.12), channel_id=1, replica_groups=mesh['y'=8,'z'=8,'c'=2,'pair'=4] {'y','z'}, dimensions={0} | all-to-all | bytes 589824 | tf_op jit(solution)/shard_map/all_to_all | solution.py:258
  34.8 0.3 phase_sum.1
  35.1 9.7 %all_to_all.16.parts = f32[8,8,512]{2,1,0:T(8,128)S(1)} all-to-all(f32[8,8,512]{2,1,0:T(8,128)S(1)} %phase_sum.1), channel_id=1, replica_groups=mesh['y'=8,'z'=8,'c'=2,'pair'=4] {'c','pair'}, dimensions={0} | all-to-all | bytes 262144 | tf_op jit(solution)/shard_map/all_to_all | solution.py:269
  44.7 0.0 copy-done
  44.7 1.5 %product.1 = (f32[16,128]{1,0:T(8,128)}, bf16[2048,128]{1,0:T(8,128)(2,1)S(1)}) custom-call(f32[8,8,512]{2,1,0:T(8,128)S(1)} %all_to_all.16.parts, bf16[4,2,256,256]{3,2,1,0:T(8,128)(2,1)S(1)} %copy-done, s32[8,128]{1,0:T(8,128)S(1)} %get-tuple-element.7.combo), custom_call_target="tpu_custom_call" | custom-call | tf_op jit(solution)/shard_map/product/pallas_call | solution.py:271
  46.2 24.6 %all_to_all.17 = bf16[64,32,128]{2,1,0:T(8,128)(2,1)S(1)} all-to-all(bf16[64,32,128]{2,1,0:T(8,128)(2,1)S(1)} %bitcast.11), channel_id=1, replica_groups=mesh['y'=8,'z'=8,'c'=2,'pair'=4] {'y','z'}, dimensions={0} | all-to-all | bytes 1048576 | tf_op jit(solution)/shard_map/all_to_all | solution.py:287
  70.8 1.1 %place.1 = bf16[8,64,4,128]{3,2,1,0:T(4,128)(2,1)} custom-call(bf16[64,8,4,128]{3,2,1,0:T(4,128)(2,1)S(1)} %bitcast.9), custom_call_target="tpu_custom_call" | custom-call | tf_op jit(solution)/shard_map/place/pallas_call | solution.py:288
Async XLA Ops:
  0.6 44.1 %copy-start = (bf16[4,2,256,256]{3,2,1,0:T(8,128)(2,1)S(1)}, bf16[4,2,256,256]{3,2,1,0:T(8,128)(2,1)}, u32[]{:S(2)}) copy-start(bf16[4,2,256,256]{3,2,1,0:T(8,128)(2,1)} %delta.1) | copy-start | bytes 3145732

commit v5 on v4

--- a/solution.py
+++ b/solution.py
@@ -133,7 +133,7 @@
     half = 2 * LANES
     re = cosine[:, :half] - sine[:, half:]
     im = cosine[:, half:] + sine[:, :half]
-    both = jnp.concatenate([re, im], axis=1)
+    both = jnp.concatenate([re, im], axis=1).astype(BF16)
     out[...] = jnp.broadcast_to(both[None], out.shape)
 
 
@@ -144,7 +144,9 @@
     pair, core = lax.axis_index("pair"), lax.axis_index("c")
     half = LANES // 2
     for q in range(4):
-        sums[q * vectors : (q + 1) * vectors, :] = (parts[q] + parts[4 + q]) * scale
+        sums[q * vectors : (q + 1) * vectors, :] = (
+            parts[q].astype(F32) + parts[4 + q].astype(F32)
+        ) * scale
     odd = (pair & 1) == 1
     lane = lax.broadcasted_iota(jnp.int32, (1, LANES), 1)
 
@@ -195,14 +197,7 @@
 
 
 def place_kernel(got, out, sems):
-    slots, chips = out.shape[:2]
-    cut = sems.shape[0] // slots
-    size = chips // cut
-    places = [
-        (got.at[i * size : (i + 1) * size, t], out.at[t, i * size : (i + 1) * size])
-        for t in range(slots)
-        for i in range(cut)
-    ]
+    places = [(got.at[:, t], out.at[t]) for t in range(out.shape[0])]
     for copy in fetch(places, sems):
         copy.wait()
 
@@ -259,7 +254,7 @@
 
     parts = pl.pallas_call(
         functools.partial(phase_kernel, kpoints, vectors),
-        out_shape=jax.ShapeDtypeStruct((cores, vectors, 2 * order), F32),
+        out_shape=jax.ShapeDtypeStruct((cores, vectors, 2 * order), BF16),
         in_specs=[VMEM],
         out_specs=VMEM,
         scratch_shapes=[pltpu.VMEM((length, LANES), F32)],
@@ -290,7 +285,7 @@
         out_shape=jax.ShapeDtypeStruct((slots, chips, 4, LANES), BF16),
         in_specs=[VMEM],
         out_specs=HBM,
-        scratch_shapes=[pltpu.SemaphoreType.DMA((4 * slots,))],
+        scratch_shapes=[pltpu.SemaphoreType.DMA((slots,))],
         compiler_params=params(),
         name="place",
     )(got.reshape(chips, slots, 4, LANES))

time: 72.1 us -> 71.7 us (level)
  no operation moved by 1% of the time
where the time goes in v5:
time: 71.7 us; the launch traced here: 71.4 us
  blocking collectives  64.9 us (91%)
  Pallas kernels  5.86 us (8%)
    all_to_all x1, blocking collectives, per_device(): lax.all_to_all(outgoing, CHIPS, split_axis=0, concat_axis=0, tiled=True)  30.9 us
    all_to_all x1, blocking collectives, per_device(): got = lax.all_to_all(sent, CHIPS, split_axis=0, concat_axis=0, tiled=True)  24.6 us
    all_to_all x1, blocking collectives, per_device(): lax.all_to_all(parts, CORES, split_axis=0, concat_axis=0, tiled=True)  9.46 us
    pallas_call x1, Pallas kernels, per_device(): pl.pallas_call(functools.partial(solve_kernel, kinds), out_shape=(jax.Sha...  3.26 us
    pallas_call x1, Pallas kernels, per_device(): pl.pallas_call(functools.partial(product_kernel, scale), out_shape=(jax.S...  1.48 us

profile of v5, /device:TPU:16, one launch (start us, length us, event | category | flops | bytes accessed | tf_op | source)
XLA Modules:
  0.0 71.4 jit_solution(740737374582017359)
XLA Ops:
  0.6 0.0 copy-start
  0.6 3.3 %solve.1 = (bf16[1152,128]{1,0:T(8,128)(2,1)S(1)}, s32[8,128]{1,0:T(8,128)S(1)}) custom-call(s32[4,3]{1,0:T(4,128)} %grid_in.1, s32[3,8]{1,0:T(4,128)} %bitcast.16, bf16[4,2,256,256]{3,2,1,0:T(8,128)(2,1)} %matrix_in.1, s32[8,128]{1,0:T(8,128)} %bitcast.14, s32[8,128]{1,0:T(8,128)} %bitcast.15, s32[1,128]{1,0:T(1,128)} %bitcast.17), custom_call_target="tpu_custom_call" | custom-call | tf_op jit(solution)/shard_map/solve/pallas_call | solution.py:231
  3.9 30.9 %all_to_all.15 = bf16[64,9,2,128]{3,2,1,0:T(2,128)(2,1)S(1)} all-to-all(bf16[64,9,2,128]{3,2,1,0:T(2,128)(2,1)S(1)} %bitcast.12), channel_id=1, replica_groups=mesh['y'=8,'z'=8,'c'=2,'pair'=4] {'y','z'}, dimensions={0} | all-to-all | bytes 589824 | tf_op jit(solution)/shard_map/all_to_all | solution.py:253
  34.8 0.3 phase_sum.1
  35.1 9.5 %all_to_all.16.parts = bf16[8,8,512]{2,1,0:T(8,128)(2,1)S(1)} all-to-all(bf16[8,8,512]{2,1,0:T(8,128)(2,1)S(1)} %phase_sum.1), channel_id=1, replica_groups=mesh['y'=8,'z'=8,'c'=2,'pair'=4] {'c','pair'}, dimensions={0} | all-to-all | bytes 131072 | tf_op jit(solution)/shard_map/all_to_all | solution.py:264
  44.5 0.0 copy-done
  44.5 1.5 %product.1 = (f32[16,128]{1,0:T(8,128)}, bf16[2048,128]{1,0:T(8,128)(2,1)S(1)}) custom-call(bf16[8,8,512]{2,1,0:T(8,128)(2,1)S(1)} %all_to_all.16.parts, bf16[4,2,256,256]{3,2,1,0:T(8,128)(2,1)S(1)} %copy-done, s32[8,128]{1,0:T(8,128)S(1)} %get-tuple-element.7.combo), custom_call_target="tpu_custom_call" | custom-call | tf_op jit(solution)/shard_map/product/pallas_call | solution.py:266
  46.0 24.6 %all_to_all.17 = bf16[64,32,128]{2,1,0:T(8,128)(2,1)S(1)} all-to-all(bf16[64,32,128]{2,1,0:T(8,128)(2,1)S(1)} %bitcast.11), channel_id=1, replica_groups=mesh['y'=8,'z'=8,'c'=2,'pair'=4] {'y','z'}, dimensions={0} | all-to-all | bytes 1048576 | tf_op jit(solution)/shard_map/all_to_all | solution.py:282
  70.6 0.8 %place.1 = bf16[8,64,4,128]{3,2,1,0:T(4,128)(2,1)} custom-call(bf16[64,8,4,128]{3,2,1,0:T(4,128)(2,1)S(1)} %bitcast.9), custom_call_target="tpu_custom_call" | custom-call | tf_op jit(solution)/shard_map/place/pallas_call | solution.py:283
Async XLA Ops:
  0.6 43.9 %copy-start = (bf16[4,2,256,256]{3,2,1,0:T(8,128)(2,1)S(1)}, bf16[4,2,256,256]{3,2,1,0:T(8,128)(2,1)}, u32[]{:S(2)}) copy-start(bf16[4,2,256,256]{3,2,1,0:T(8,128)(2,1)} %delta.1) | copy-start | bytes 3145732

commit v6 on v5

--- a/solution.py
+++ b/solution.py
@@ -43,17 +43,17 @@
 
 
 def solve_kernel(
-    kinds, grid_in, lattice_in, matrix_in, route_in, species_in, count_in, out, combo, *scratch
+    kinds, grid_in, lattice_in, matrix_in, route_in, species_in, count_in, out, chosen, *scratch
 ):
     grid, lattice, matrix, route, species, count, wide, sems = scratch
     kpoints, _, order, _ = matrix.shape
     own = order // 4
     chunk = out.shape[0] // own
     places = [(matrix_in.at[k, i], matrix.at[k, i]) for k in range(kpoints) for i in range(2)]
-    places = [(grid_in, grid), (lattice_in, lattice)] + places
-    places += [(route_in, route), (species_in, species), (count_in, count)]
-    copies = fetch(places, sems)
-    small, large, late = copies[:2], copies[2:-3], copies[-3:]
+    small = [(grid_in, grid), (lattice_in, lattice), (route_in, route), (species_in, species)]
+    small += [(count_in, count)]
+    copies = fetch(small + places, sems)
+    small, large = copies[: len(small)], copies[len(small) :]
     for copy in small:
         copy.wait()
     vectors = lattice.shape[1]
@@ -76,6 +76,19 @@
     phase = jnp.broadcast_to(phase[:1], (own, LANES))
     wide[pl.ds(chunk - 2, own, stride=chunk), :] = phase
     wide[pl.ds(chunk - 1, own, stride=chunk), :] = jnp.zeros((own, LANES), F32)
+    slots, owners = route.shape
+    chips = owners // 2
+    alive = lax.broadcasted_iota(jnp.int32, (slots, owners), 0) < count[...]
+    combo = jnp.where(alive, species[...] * vectors + route[...], kinds * vectors)
+    combo = jnp.transpose(combo.astype(F32)).astype(BF16)
+    row = lax.broadcasted_iota(jnp.int32, (chips, owners), 0)
+    col = lax.broadcasted_iota(jnp.int32, (chips, owners), 1)
+    mine = jnp.where(col == row * 2 + lax.axis_index("c"), 1.0, 0.0).astype(BF16)
+    combo = dot(mine, combo)
+    which = lax.broadcasted_iota(jnp.int32, (chips, kinds * vectors), 1).astype(F32)
+    for t in range(slots):
+        hit = jnp.broadcast_to(combo[:, t : t + 1], which.shape) == which
+        chosen[t * chips : (t + 1) * chips, :] = jnp.where(hit, 1.0, 0.0).astype(BF16)
     row = lax.broadcasted_iota(jnp.int32, (own, order), 0)
     col = lax.broadcasted_iota(jnp.int32, (own, order), 1)
     pick = jnp.where(col == row * 4 + lax.axis_index("pair"), 1.0, 0.0).astype(BF16)
@@ -110,10 +123,6 @@
                 wide[pl.ds(place, own, stride=chunk), :] = now[k][part][
                     :, half * LANES : (half + 1) * LANES
                 ]
-    for copy in late:
-        copy.wait()
-    alive = lax.broadcasted_iota(jnp.int32, combo.shape, 0) < count[...]
-    combo[...] = jnp.where(alive, species[...] * vectors + route[...], kinds * vectors)
     out[...] = wide[...].astype(BF16)
 
 
@@ -133,20 +142,17 @@
     half = 2 * LANES
     re = cosine[:, :half] - sine[:, half:]
     im = cosine[:, half:] + sine[:, :half]
-    both = jnp.concatenate([re, im], axis=1).astype(BF16)
+    both = jnp.concatenate([re, im], axis=1)
     out[...] = jnp.broadcast_to(both[None], out.shape)
 
 
-def product_kernel(scale, parts, delta, combo, host, out, wide, sums):
+def product_kernel(scale, slots, parts, delta, chosen, host, out, wide, sums):
     vectors = parts.shape[1]
     kinds, _, order, _ = delta.shape
-    slots, owners = combo.shape
     pair, core = lax.axis_index("pair"), lax.axis_index("c")
     half = LANES // 2
     for q in range(4):
-        sums[q * vectors : (q + 1) * vectors, :] = (
-            parts[q].astype(F32) + parts[4 + q].astype(F32)
-        ) * scale
+        sums[q * vectors : (q + 1) * vectors, :] = (parts[q] + parts[4 + q]) * scale
     odd = (pair & 1) == 1
     lane = lax.broadcasted_iota(jnp.int32, (1, LANES), 1)
 
@@ -176,18 +182,8 @@
             jnp.concatenate([product[q * vectors : (q + 1) * vectors] for q in range(4)], axis=1)
         )
     table = jnp.concatenate(table, axis=0).astype(BF16)
-    combo = jnp.transpose(combo[...].astype(F32)).astype(BF16)
-    chips = owners // 2
-    row = lax.broadcasted_iota(jnp.int32, (chips, owners), 0)
-    col = lax.broadcasted_iota(jnp.int32, (chips, owners), 1)
-    combo = dot(jnp.where(col == row * 2 + core, 1.0, 0.0).astype(BF16), combo)
-    kind = lax.broadcasted_iota(jnp.int32, (chips, kinds * vectors), 1).astype(F32)
-    chosen = [
-        jnp.where(jnp.broadcast_to(combo[:, t : t + 1], kind.shape) == kind, 1.0, 0.0)
-        for t in range(slots)
-    ]
-    chosen = jnp.concatenate(chosen, axis=0).astype(BF16)
-    picked = dot(chosen, table)
+    chips = chosen.shape[0] // slots
+    picked = dot(chosen[...], table)
     for t in range(slots):
         for q in range(4):
             wide[pl.ds(t * 4 + q, chips, stride=4 * slots), :] = picked[
@@ -228,11 +224,11 @@
     length = chips * chunk
 
     route, kind, count = pair_route.T, species.T, pair_count[None]
-    outgoing, combo = pl.pallas_call(
+    outgoing, chosen = pl.pallas_call(
         functools.partial(solve_kernel, kinds),
         out_shape=(
             jax.ShapeDtypeStruct((length, LANES), BF16),
-            jax.ShapeDtypeStruct(route.shape, jnp.int32),
+            jax.ShapeDtypeStruct((chips * slots, kinds * vectors), BF16),
         ),
         in_specs=[HBM] * 6,
         out_specs=(VMEM, VMEM),
@@ -254,7 +250,7 @@
 
     parts = pl.pallas_call(
         functools.partial(phase_kernel, kpoints, vectors),
-        out_shape=jax.ShapeDtypeStruct((cores, vectors, 2 * order), BF16),
+        out_shape=jax.ShapeDtypeStruct((cores, vectors, 2 * order), F32),
         in_specs=[VMEM],
         out_specs=VMEM,
         scratch_shapes=[pltpu.VMEM((length, LANES), F32)],
@@ -264,7 +260,7 @@
     parts = lax.all_to_all(parts, CORES, split_axis=0, concat_axis=0, tiled=True)
 
     host_rows, sent = pl.pallas_call(
-        functools.partial(product_kernel, scale),
+        functools.partial(product_kernel, scale, slots),
         out_shape=(
             jax.ShapeDtypeStruct((2 * vectors, LANES), F32),
             jax.ShapeDtypeStruct((chips * slots * 4, LANES), BF16),
@@ -277,7 +273,7 @@
         ],
         compiler_params=params(),
         name="product",
-    )(parts, delta_t, combo)
+    )(parts, delta_t, chosen)
     sent = sent.reshape(chips, slots * 4, LANES)
     got = lax.all_to_all(sent, CHIPS, split_axis=0, concat_axis=0, tiled=True)
     cluster = pl.pallas_call(

time: 71.7 us -> 72.1 us (level)
  no operation moved by 1% of the time
where the time goes in v6:
time: 72.1 us; the launch traced here: 71.8 us
  blocking collectives  65.1 us (90%)
  Pallas kernels  6.07 us (8%)
    all_to_all x1, blocking collectives, per_device(): lax.all_to_all(outgoing, CHIPS, split_axis=0, concat_axis=0, tiled=True)  30.9 us
    all_to_all x1, blocking collectives, per_device(): got = lax.all_to_all(sent, CHIPS, split_axis=0, concat_axis=0, tiled=True)  24.6 us
    all_to_all x1, blocking collectives, per_device(): lax.all_to_all(parts, CORES, split_axis=0, concat_axis=0, tiled=True)  9.65 us
    pallas_call x1, Pallas kernels, per_device(): pl.pallas_call(functools.partial(solve_kernel, kinds), out_shape=(jax.Sha...  3.48 us
    pallas_call x1, Pallas kernels, per_device(): pl.pallas_call(functools.partial(product_kernel, scale, slots), out_shape...  1.47 us

profile of v6, /device:TPU:16, one launch (start us, length us, event | category | flops | bytes accessed | tf_op | source)
XLA Modules:
  0.0 71.8 jit_solution(18390176359074833251)
XLA Ops:
  0.6 0.0 copy-start
  0.6 3.5 %solve.1 = (bf16[1152,128]{1,0:T(8,128)(2,1)S(1)}, bf16[512,32]{1,0:T(8,128)(2,1)S(1)}) custom-call(s32[4,3]{1,0:T(4,128)} %grid_in.1, s32[3,8]{1,0:T(4,128)} %bitcast.16, bf16[4,2,256,256]{3,2,1,0:T(8,128)(2,1)} %matrix_in.1, s32[8,128]{1,0:T(8,128)} %bitcast.14, s32[8,128]{1,0:T(8,128)} %bitcast.15, s32[1,128]{1,0:T(1,128)} %bitcast.17), custom_call_target="tpu_custom_call" | custom-call | tf_op jit(solution)/shard_map/solve/pallas_call | solution.py:227
  4.1 30.9 %all_to_all.15 = bf16[64,9,2,128]{3,2,1,0:T(2,128)(2,1)S(1)} all-to-all(bf16[64,9,2,128]{3,2,1,0:T(2,128)(2,1)S(1)} %bitcast.12), channel_id=1, replica_groups=mesh['y'=8,'z'=8,'c'=2,'pair'=4] {'y','z'}, dimensions={0} | all-to-all | bytes 589824 | tf_op jit(solution)/shard_map/all_to_all | solution.py:249
  35.0 0.3 phase_sum.1
  35.3 9.7 %all_to_all.16.parts = f32[8,8,512]{2,1,0:T(8,128)S(1)} all-to-all(f32[8,8,512]{2,1,0:T(8,128)S(1)} %phase_sum.1), channel_id=1, replica_groups=mesh['y'=8,'z'=8,'c'=2,'pair'=4] {'c','pair'}, dimensions={0} | all-to-all | bytes 262144 | tf_op jit(solution)/shard_map/all_to_all | solution.py:260
  45.0 0.0 copy-done
  45.0 1.5 %product.1 = (f32[16,128]{1,0:T(8,128)}, bf16[2048,128]{1,0:T(8,128)(2,1)S(1)}) custom-call(f32[8,8,512]{2,1,0:T(8,128)S(1)} %all_to_all.16.parts, bf16[4,2,256,256]{3,2,1,0:T(8,128)(2,1)S(1)} %copy-done, bf16[512,32]{1,0:T(8,128)(2,1)S(1)} %get-tuple-element.7.chosen), custom_call_target="tpu_custom_call" | custom-call | tf_op jit(solution)/shard_map/product/pallas_call | solution.py:262
  46.4 24.6 %all_to_all.17 = bf16[64,32,128]{2,1,0:T(8,128)(2,1)S(1)} all-to-all(bf16[64,32,128]{2,1,0:T(8,128)(2,1)S(1)} %bitcast.11), channel_id=1, replica_groups=mesh['y'=8,'z'=8,'c'=2,'pair'=4] {'y','z'}, dimensions={0} | all-to-all | bytes 1048576 | tf_op jit(solution)/shard_map/all_to_all | solution.py:278
  71.0 0.8 %place.1 = bf16[8,64,4,128]{3,2,1,0:T(4,128)(2,1)} custom-call(bf16[64,8,4,128]{3,2,1,0:T(4,128)(2,1)S(1)} %bitcast.9), custom_call_target="tpu_custom_call" | custom-call | tf_op jit(solution)/shard_map/place/pallas_call | solution.py:279
Async XLA Ops:
  0.6 44.3 %copy-start = (bf16[4,2,256,256]{3,2,1,0:T(8,128)(2,1)S(1)}, bf16[4,2,256,256]{3,2,1,0:T(8,128)(2,1)}, u32[]{:S(2)}) copy-start(bf16[4,2,256,256]{3,2,1,0:T(8,128)(2,1)} %delta.1) | copy-start | bytes 3145732

commit v7 on v5

--- a/solution.py
+++ b/solution.py
@@ -133,20 +133,18 @@
     half = 2 * LANES
     re = cosine[:, :half] - sine[:, half:]
     im = cosine[:, half:] + sine[:, :half]
-    both = jnp.concatenate([re, im], axis=1).astype(BF16)
+    both = jnp.concatenate([re, im], axis=1)
     out[...] = jnp.broadcast_to(both[None], out.shape)
 
 
-def product_kernel(scale, parts, delta, combo, host, out, wide, sums):
+def product_kernel(scale, parts, delta, combo, host, out, wide, sums, chosen):
     vectors = parts.shape[1]
     kinds, _, order, _ = delta.shape
     slots, owners = combo.shape
     pair, core = lax.axis_index("pair"), lax.axis_index("c")
     half = LANES // 2
     for q in range(4):
-        sums[q * vectors : (q + 1) * vectors, :] = (
-            parts[q].astype(F32) + parts[4 + q].astype(F32)
-        ) * scale
+        sums[q * vectors : (q + 1) * vectors, :] = (parts[q] + parts[4 + q]) * scale
     odd = (pair & 1) == 1
     lane = lax.broadcasted_iota(jnp.int32, (1, LANES), 1)
 
@@ -181,18 +179,14 @@
     row = lax.broadcasted_iota(jnp.int32, (chips, owners), 0)
     col = lax.broadcasted_iota(jnp.int32, (chips, owners), 1)
     combo = dot(jnp.where(col == row * 2 + core, 1.0, 0.0).astype(BF16), combo)
-    kind = lax.broadcasted_iota(jnp.int32, (chips, kinds * vectors), 1).astype(F32)
-    chosen = [
-        jnp.where(jnp.broadcast_to(combo[:, t : t + 1], kind.shape) == kind, 1.0, 0.0)
-        for t in range(slots)
-    ]
-    chosen = jnp.concatenate(chosen, axis=0).astype(BF16)
+    kind = lax.broadcasted_iota(jnp.int32, (chips, LANES), 1).astype(F32)
+    for t in range(slots):
+        hit = jnp.broadcast_to(combo[:, t : t + 1], kind.shape) == kind
+        chosen[pl.ds(t, chips, stride=slots), :] = jnp.where(hit, 1.0, 0.0)
+    chosen = chosen[:, : kinds * vectors].astype(BF16)
     picked = dot(chosen, table)
-    for t in range(slots):
-        for q in range(4):
-            wide[pl.ds(t * 4 + q, chips, stride=4 * slots), :] = picked[
-                t * chips : (t + 1) * chips, q * LANES : (q + 1) * LANES
-            ]
+    for q in range(4):
+        wide[pl.ds(q, chips * slots, stride=4), :] = picked[:, q * LANES : (q + 1) * LANES]
     out[...] = wide[...].astype(BF16)
 
 
@@ -254,7 +248,7 @@
 
     parts = pl.pallas_call(
         functools.partial(phase_kernel, kpoints, vectors),
-        out_shape=jax.ShapeDtypeStruct((cores, vectors, 2 * order), BF16),
+        out_shape=jax.ShapeDtypeStruct((cores, vectors, 2 * order), F32),
         in_specs=[VMEM],
         out_specs=VMEM,
         scratch_shapes=[pltpu.VMEM((length, LANES), F32)],
@@ -274,6 +268,7 @@
         scratch_shapes=[
             pltpu.VMEM((chips * slots * 4, LANES), F32),
             pltpu.VMEM((4 * vectors, 2 * order), F32),
+            pltpu.VMEM((chips * slots, LANES), F32),
         ],
         compiler_params=params(),
         name="product",

time: 71.7 us -> 71.6 us (level)
  no operation moved by 1% of the time
where the time goes in v7:
time: 71.6 us; the launch traced here: 71.4 us
  blocking collectives  65.1 us (91%)
  Pallas kernels  5.63 us (8%)
    all_to_all x1, blocking collectives, per_device(): lax.all_to_all(outgoing, CHIPS, split_axis=0, concat_axis=0, tiled=True)  30.9 us
    all_to_all x1, blocking collectives, per_device(): got = lax.all_to_all(sent, CHIPS, split_axis=0, concat_axis=0, tiled=True)  24.6 us
    all_to_all x1, blocking collectives, per_device(): lax.all_to_all(parts, CORES, split_axis=0, concat_axis=0, tiled=True)  9.66 us
    pallas_call x1, Pallas kernels, per_device(): pl.pallas_call(functools.partial(solve_kernel, kinds), out_shape=(jax.Sha...  3.26 us

profile of v7, /device:TPU:16, one launch (start us, length us, event | category | flops | bytes accessed | tf_op | source)
XLA Modules:
  0.0 71.4 jit_solution(17609746497891101689)
XLA Ops:
  0.6 0.0 copy-start
  0.6 3.3 %solve.1 = (bf16[1152,128]{1,0:T(8,128)(2,1)S(1)}, s32[8,128]{1,0:T(8,128)S(1)}) custom-call(s32[4,3]{1,0:T(4,128)} %grid_in.1, s32[3,8]{1,0:T(4,128)} %bitcast.16, bf16[4,2,256,256]{3,2,1,0:T(8,128)(2,1)} %matrix_in.1, s32[8,128]{1,0:T(8,128)} %bitcast.14, s32[8,128]{1,0:T(8,128)} %bitcast.15, s32[1,128]{1,0:T(1,128)} %bitcast.17), custom_call_target="tpu_custom_call" | custom-call | tf_op jit(solution)/shard_map/solve/pallas_call | solution.py:225
  3.9 30.9 %all_to_all.15 = bf16[64,9,2,128]{3,2,1,0:T(2,128)(2,1)S(1)} all-to-all(bf16[64,9,2,128]{3,2,1,0:T(2,128)(2,1)S(1)} %bitcast.12), channel_id=1, replica_groups=mesh['y'=8,'z'=8,'c'=2,'pair'=4] {'y','z'}, dimensions={0} | all-to-all | bytes 589824 | tf_op jit(solution)/shard_map/all_to_all | solution.py:247
  34.8 0.3 phase_sum.1
  35.1 9.7 %all_to_all.16.parts = f32[8,8,512]{2,1,0:T(8,128)S(1)} all-to-all(f32[8,8,512]{2,1,0:T(8,128)S(1)} %phase_sum.1), channel_id=1, replica_groups=mesh['y'=8,'z'=8,'c'=2,'pair'=4] {'c','pair'}, dimensions={0} | all-to-all | bytes 262144 | tf_op jit(solution)/shard_map/all_to_all | solution.py:258
  44.7 0.0 copy-done
  44.7 1.2 %product.1 = (f32[16,128]{1,0:T(8,128)}, bf16[2048,128]{1,0:T(8,128)(2,1)S(1)}) custom-call(f32[8,8,512]{2,1,0:T(8,128)S(1)} %all_to_all.16.parts, bf16[4,2,256,256]{3,2,1,0:T(8,128)(2,1)S(1)} %copy-done, s32[8,128]{1,0:T(8,128)S(1)} %get-tuple-element.7.combo), custom_call_target="tpu_custom_call" | custom-call | tf_op jit(solution)/shard_map/product/pallas_call | solution.py:260
  46.0 24.6 %all_to_all.17 = bf16[64,32,128]{2,1,0:T(8,128)(2,1)S(1)} all-to-all(bf16[64,32,128]{2,1,0:T(8,128)(2,1)S(1)} %bitcast.11), channel_id=1, replica_groups=mesh['y'=8,'z'=8,'c'=2,'pair'=4] {'y','z'}, dimensions={0} | all-to-all | bytes 1048576 | tf_op jit(solution)/shard_map/all_to_all | solution.py:277
  70.6 0.8 %place.1 = bf16[8,64,4,128]{3,2,1,0:T(4,128)(2,1)} custom-call(bf16[64,8,4,128]{3,2,1,0:T(4,128)(2,1)S(1)} %bitcast.9), custom_call_target="tpu_custom_call" | custom-call | tf_op jit(solution)/shard_map/place/pallas_call | solution.py:278
Async XLA Ops:
  0.6 44.1 %copy-start = (bf16[4,2,256,256]{3,2,1,0:T(8,128)(2,1)S(1)}, bf16[4,2,256,256]{3,2,1,0:T(8,128)(2,1)}, u32[]{:S(2)}) copy-start(bf16[4,2,256,256]{3,2,1,0:T(8,128)(2,1)} %delta.1) | copy-start | bytes 3145732

commit v8 on v7

--- a/solution.py
+++ b/solution.py
@@ -49,7 +49,12 @@
     kpoints, _, order, _ = matrix.shape
     own = order // 4
     chunk = out.shape[0] // own
-    places = [(matrix_in.at[k, i], matrix.at[k, i]) for k in range(kpoints) for i in range(2)]
+    places = [
+        (matrix_in.at[k, i, j : j + order // 2], matrix.at[k, i, j : j + order // 2])
+        for k in range(kpoints)
+        for i in range(2)
+        for j in (0, order // 2)
+    ]
     places = [(grid_in, grid), (lattice_in, lattice)] + places
     places += [(route_in, route), (species_in, species), (count_in, count)]
     copies = fetch(places, sems)
@@ -81,8 +86,8 @@
     pick = jnp.where(col == row * 4 + lax.axis_index("pair"), 1.0, 0.0).astype(BF16)
     first = []
     for k in range(kpoints):
-        large[2 * k].wait()
-        large[2 * k + 1].wait()
+        for copy in large[4 * k : 4 * k + 4]:
+            copy.wait()
         first.append([dot(pick, matrix[k, part]) for part in range(2)])
     now = [list(pair) for pair in first]
     for step in range(ITERS - 1):
@@ -133,7 +138,7 @@
     half = 2 * LANES
     re = cosine[:, :half] - sine[:, half:]
     im = cosine[:, half:] + sine[:, :half]
-    both = jnp.concatenate([re, im], axis=1)
+    both = jnp.concatenate([re, im], axis=1).astype(BF16)
     out[...] = jnp.broadcast_to(both[None], out.shape)
 
 
@@ -144,7 +149,9 @@
     pair, core = lax.axis_index("pair"), lax.axis_index("c")
     half = LANES // 2
     for q in range(4):
-        sums[q * vectors : (q + 1) * vectors, :] = (parts[q] + parts[4 + q]) * scale
+        sums[q * vectors : (q + 1) * vectors, :] = (
+            parts[q].astype(F32) + parts[4 + q].astype(F32)
+        ) * scale
     odd = (pair & 1) == 1
     lane = lax.broadcasted_iota(jnp.int32, (1, LANES), 1)
 
@@ -238,7 +245,7 @@
             pltpu.VMEM(kind.shape, jnp.int32),
             pltpu.VMEM(count.shape, jnp.int32),
             pltpu.VMEM((length, LANES), F32),
-            pltpu.SemaphoreType.DMA((2 * kpoints + 5,)),
+            pltpu.SemaphoreType.DMA((4 * kpoints + 5,)),
         ],
         compiler_params=params(),
         name="solve",
@@ -248,7 +255,7 @@
 
     parts = pl.pallas_call(
         functools.partial(phase_kernel, kpoints, vectors),
-        out_shape=jax.ShapeDtypeStruct((cores, vectors, 2 * order), F32),
+        out_shape=jax.ShapeDtypeStruct((cores, vectors, 2 * order), BF16),
         in_specs=[VMEM],
         out_specs=VMEM,
         scratch_shapes=[pltpu.VMEM((length, LANES), F32)],

time: 71.6 us -> 71.5 us (level)
  no operation moved by 1% of the time
where the time goes in v8:
time: 71.5 us; the launch traced here: 71.2 us
  blocking collectives  64.9 us (91%)
  Pallas kernels  5.66 us (8%)
    all_to_all x1, blocking collectives, per_device(): lax.all_to_all(outgoing, CHIPS, split_axis=0, concat_axis=0, tiled=True)  30.9 us
    all_to_all x1, blocking collectives, per_device(): got = lax.all_to_all(sent, CHIPS, split_axis=0, concat_axis=0, tiled=True)  24.6 us
    all_to_all x1, blocking collectives, per_device(): lax.all_to_all(parts, CORES, split_axis=0, concat_axis=0, tiled=True)  9.46 us
    pallas_call x1, Pallas kernels, per_device(): pl.pallas_call(functools.partial(solve_kernel, kinds), out_shape=(jax.Sha...  3.3 us

profile of v8, /device:TPU:16, one launch (start us, length us, event | category | flops | bytes accessed | tf_op | source)
XLA Modules:
  0.0 71.2 jit_solution(12308902508646114795)
XLA Ops:
  0.6 0.0 copy-start
  0.6 3.3 %solve.1 = (bf16[1152,128]{1,0:T(8,128)(2,1)S(1)}, s32[8,128]{1,0:T(8,128)S(1)}) custom-call(s32[4,3]{1,0:T(4,128)} %grid_in.1, s32[3,8]{1,0:T(4,128)} %bitcast.16, bf16[4,2,256,256]{3,2,1,0:T(8,128)(2,1)} %matrix_in.1, s32[8,128]{1,0:T(8,128)} %bitcast.14, s32[8,128]{1,0:T(8,128)} %bitcast.15, s32[1,128]{1,0:T(1,128)} %bitcast.17), custom_call_target="tpu_custom_call" | custom-call | tf_op jit(solution)/shard_map/solve/pallas_call | solution.py:232
  3.9 30.9 %all_to_all.15 = bf16[64,9,2,128]{3,2,1,0:T(2,128)(2,1)S(1)} all-to-all(bf16[64,9,2,128]{3,2,1,0:T(2,128)(2,1)S(1)} %bitcast.12), channel_id=1, replica_groups=mesh['y'=8,'z'=8,'c'=2,'pair'=4] {'y','z'}, dimensions={0} | all-to-all | bytes 589824 | tf_op jit(solution)/shard_map/all_to_all | solution.py:254
  34.8 0.3 phase_sum.1
  35.1 9.5 %all_to_all.16.parts = bf16[8,8,512]{2,1,0:T(8,128)(2,1)S(1)} all-to-all(bf16[8,8,512]{2,1,0:T(8,128)(2,1)S(1)} %phase_sum.1), channel_id=1, replica_groups=mesh['y'=8,'z'=8,'c'=2,'pair'=4] {'c','pair'}, dimensions={0} | all-to-all | bytes 131072 | tf_op jit(solution)/shard_map/all_to_all | solution.py:265
  44.6 0.0 copy-done
  44.6 1.2 %product.1 = (f32[16,128]{1,0:T(8,128)}, bf16[2048,128]{1,0:T(8,128)(2,1)S(1)}) custom-call(bf16[8,8,512]{2,1,0:T(8,128)(2,1)S(1)} %all_to_all.16.parts, bf16[4,2,256,256]{3,2,1,0:T(8,128)(2,1)S(1)} %copy-done, s32[8,128]{1,0:T(8,128)S(1)} %get-tuple-element.7.combo), custom_call_target="tpu_custom_call" | custom-call | tf_op jit(solution)/shard_map/product/pallas_call | solution.py:267
  45.8 24.6 %all_to_all.17 = bf16[64,32,128]{2,1,0:T(8,128)(2,1)S(1)} all-to-all(bf16[64,32,128]{2,1,0:T(8,128)(2,1)S(1)} %bitcast.11), channel_id=1, replica_groups=mesh['y'=8,'z'=8,'c'=2,'pair'=4] {'y','z'}, dimensions={0} | all-to-all | bytes 1048576 | tf_op jit(solution)/shard_map/all_to_all | solution.py:284
  70.4 0.8 %place.1 = bf16[8,64,4,128]{3,2,1,0:T(4,128)(2,1)} custom-call(bf16[64,8,4,128]{3,2,1,0:T(4,128)(2,1)S(1)} %bitcast.9), custom_call_target="tpu_custom_call" | custom-call | tf_op jit(solution)/shard_map/place/pallas_call | solution.py:285
Async XLA Ops:
  0.6 44.0 %copy-start = (bf16[4,2,256,256]{3,2,1,0:T(8,128)(2,1)S(1)}, bf16[4,2,256,256]{3,2,1,0:T(8,128)(2,1)}, u32[]{:S(2)}) copy-start(bf16[4,2,256,256]{3,2,1,0:T(8,128)(2,1)} %delta.1) | copy-start | bytes 3145732

commit v9 on v7

--- a/solution.py
+++ b/solution.py
@@ -133,7 +133,7 @@
     half = 2 * LANES
     re = cosine[:, :half] - sine[:, half:]
     im = cosine[:, half:] + sine[:, :half]
-    both = jnp.concatenate([re, im], axis=1)
+    both = jnp.concatenate([re, im], axis=1).astype(BF16)
     out[...] = jnp.broadcast_to(both[None], out.shape)
 
 
@@ -144,7 +144,9 @@
     pair, core = lax.axis_index("pair"), lax.axis_index("c")
     half = LANES // 2
     for q in range(4):
-        sums[q * vectors : (q + 1) * vectors, :] = (parts[q] + parts[4 + q]) * scale
+        sums[q * vectors : (q + 1) * vectors, :] = (
+            parts[q].astype(F32) + parts[4 + q].astype(F32)
+        ) * scale
     odd = (pair & 1) == 1
     lane = lax.broadcasted_iota(jnp.int32, (1, LANES), 1)
 
@@ -248,7 +250,7 @@
 
     parts = pl.pallas_call(
         functools.partial(phase_kernel, kpoints, vectors),
-        out_shape=jax.ShapeDtypeStruct((cores, vectors, 2 * order), F32),
+        out_shape=jax.ShapeDtypeStruct((cores, vectors, 2 * order), BF16),
         in_specs=[VMEM],
         out_specs=VMEM,
         scratch_shapes=[pltpu.VMEM((length, LANES), F32)],

time: 71.6 us -> 71.4 us (level)
  no operation moved by 1% of the time
where the time goes in v9:
time: 71.4 us; the launch traced here: 71.2 us
  blocking collectives  64.9 us (91%)
  Pallas kernels  5.62 us (8%)
    all_to_all x1, blocking collectives, per_device(): lax.all_to_all(outgoing, CHIPS, split_axis=0, concat_axis=0, tiled=True)  30.9 us
    all_to_all x1, blocking collectives, per_device(): got = lax.all_to_all(sent, CHIPS, split_axis=0, concat_axis=0, tiled=True)  24.6 us
    all_to_all x1, blocking collectives, per_device(): lax.all_to_all(parts, CORES, split_axis=0, concat_axis=0, tiled=True)  9.46 us
    pallas_call x1, Pallas kernels, per_device(): pl.pallas_call(functools.partial(solve_kernel, kinds), out_shape=(jax.Sha...  3.26 us

profile of v9, /device:TPU:16, one launch (start us, length us, event | category | flops | bytes accessed | tf_op | source)
XLA Modules:
  0.0 71.2 jit_solution(1811528969751443779)
XLA Ops:
  0.6 0.0 copy-start
  0.6 3.3 %solve.1 = (bf16[1152,128]{1,0:T(8,128)(2,1)S(1)}, s32[8,128]{1,0:T(8,128)S(1)}) custom-call(s32[4,3]{1,0:T(4,128)} %grid_in.1, s32[3,8]{1,0:T(4,128)} %bitcast.16, bf16[4,2,256,256]{3,2,1,0:T(8,128)(2,1)} %matrix_in.1, s32[8,128]{1,0:T(8,128)} %bitcast.14, s32[8,128]{1,0:T(8,128)} %bitcast.15, s32[1,128]{1,0:T(1,128)} %bitcast.17), custom_call_target="tpu_custom_call" | custom-call | tf_op jit(solution)/shard_map/solve/pallas_call | solution.py:227
  3.9 30.9 %all_to_all.15 = bf16[64,9,2,128]{3,2,1,0:T(2,128)(2,1)S(1)} all-to-all(bf16[64,9,2,128]{3,2,1,0:T(2,128)(2,1)S(1)} %bitcast.12), channel_id=1, replica_groups=mesh['y'=8,'z'=8,'c'=2,'pair'=4] {'y','z'}, dimensions={0} | all-to-all | bytes 589824 | tf_op jit(solution)/shard_map/all_to_all | solution.py:249
  34.8 0.3 phase_sum.1
  35.1 9.5 %all_to_all.16.parts = bf16[8,8,512]{2,1,0:T(8,128)(2,1)S(1)} all-to-all(bf16[8,8,512]{2,1,0:T(8,128)(2,1)S(1)} %phase_sum.1), channel_id=1, replica_groups=mesh['y'=8,'z'=8,'c'=2,'pair'=4] {'c','pair'}, dimensions={0} | all-to-all | bytes 131072 | tf_op jit(solution)/shard_map/all_to_all | solution.py:260
  44.5 0.0 copy-done
  44.5 1.2 %product.1 = (f32[16,128]{1,0:T(8,128)}, bf16[2048,128]{1,0:T(8,128)(2,1)S(1)}) custom-call(bf16[8,8,512]{2,1,0:T(8,128)(2,1)S(1)} %all_to_all.16.parts, bf16[4,2,256,256]{3,2,1,0:T(8,128)(2,1)S(1)} %copy-done, s32[8,128]{1,0:T(8,128)S(1)} %get-tuple-element.7.combo), custom_call_target="tpu_custom_call" | custom-call | tf_op jit(solution)/shard_map/product/pallas_call | solution.py:262
  45.8 24.6 %all_to_all.17 = bf16[64,32,128]{2,1,0:T(8,128)(2,1)S(1)} all-to-all(bf16[64,32,128]{2,1,0:T(8,128)(2,1)S(1)} %bitcast.11), channel_id=1, replica_groups=mesh['y'=8,'z'=8,'c'=2,'pair'=4] {'y','z'}, dimensions={0} | all-to-all | bytes 1048576 | tf_op jit(solution)/shard_map/all_to_all | solution.py:279
  70.4 0.8 %place.1 = bf16[8,64,4,128]{3,2,1,0:T(4,128)(2,1)} custom-call(bf16[64,8,4,128]{3,2,1,0:T(4,128)(2,1)S(1)} %bitcast.9), custom_call_target="tpu_custom_call" | custom-call | tf_op jit(solution)/shard_map/place/pallas_call | solution.py:280
Async XLA Ops:
  0.6 43.9 %copy-start = (bf16[4,2,256,256]{3,2,1,0:T(8,128)(2,1)S(1)}, bf16[4,2,256,256]{3,2,1,0:T(8,128)(2,1)}, u32[]{:S(2)}) copy-start(bf16[4,2,256,256]{3,2,1,0:T(8,128)(2,1)} %delta.1) | copy-start | bytes 3145732

commit v10 on v9

--- a/solution.py
+++ b/solution.py
@@ -49,7 +49,7 @@
     kpoints, _, order, _ = matrix.shape
     own = order // 4
     chunk = out.shape[0] // own
-    places = [(matrix_in.at[k, i], matrix.at[k, i]) for k in range(kpoints) for i in range(2)]
+    places = [(matrix_in.at[k], matrix.at[k]) for k in range(kpoints)]
     places = [(grid_in, grid), (lattice_in, lattice)] + places
     places += [(route_in, route), (species_in, species), (count_in, count)]
     copies = fetch(places, sems)
@@ -81,8 +81,7 @@
     pick = jnp.where(col == row * 4 + lax.axis_index("pair"), 1.0, 0.0).astype(BF16)
     first = []
     for k in range(kpoints):
-        large[2 * k].wait()
-        large[2 * k + 1].wait()
+        large[k].wait()
         first.append([dot(pick, matrix[k, part]) for part in range(2)])
     now = [list(pair) for pair in first]
     for step in range(ITERS - 1):
@@ -240,7 +239,7 @@
             pltpu.VMEM(kind.shape, jnp.int32),
             pltpu.VMEM(count.shape, jnp.int32),
             pltpu.VMEM((length, LANES), F32),
-            pltpu.SemaphoreType.DMA((2 * kpoints + 5,)),
+            pltpu.SemaphoreType.DMA((kpoints + 5,)),
         ],
         compiler_params=params(),
         name="solve",

time: 71.4 us -> 71.4 us (level)
  no operation moved by 1% of the time
where the time goes in v10:
time: 71.4 us; the launch traced here: 71.1 us
  blocking collectives  64.9 us (91%)
  Pallas kernels  5.56 us (8%)
    all_to_all x1, blocking collectives, per_device(): lax.all_to_all(outgoing, CHIPS, split_axis=0, concat_axis=0, tiled=True)  30.9 us
    all_to_all x1, blocking collectives, per_device(): got = lax.all_to_all(sent, CHIPS, split_axis=0, concat_axis=0, tiled=True)  24.6 us
    all_to_all x1, blocking collectives, per_device(): lax.all_to_all(parts, CORES, split_axis=0, concat_axis=0, tiled=True)  9.45 us
    pallas_call x1, Pallas kernels, per_device(): pl.pallas_call(functools.partial(solve_kernel, kinds), out_shape=(jax.Sha...  3.2 us

profile of v10, /device:TPU:16, one launch (start us, length us, event | category | flops | bytes accessed | tf_op | source)
XLA Modules:
  0.0 71.1 jit_solution(11089069196755616669)
XLA Ops:
  0.6 0.0 copy-start
  0.6 3.2 %solve.1 = (bf16[1152,128]{1,0:T(8,128)(2,1)S(1)}, s32[8,128]{1,0:T(8,128)S(1)}) custom-call(s32[4,3]{1,0:T(4,128)} %grid_in.1, s32[3,8]{1,0:T(4,128)} %bitcast.16, bf16[4,2,256,256]{3,2,1,0:T(8,128)(2,1)} %matrix_in.1, s32[8,128]{1,0:T(8,128)} %bitcast.14, s32[8,128]{1,0:T(8,128)} %bitcast.15, s32[1,128]{1,0:T(1,128)} %bitcast.17), custom_call_target="tpu_custom_call" | custom-call | tf_op jit(solution)/shard_map/solve/pallas_call | solution.py:226
  3.9 30.9 %all_to_all.15 = bf16[64,9,2,128]{3,2,1,0:T(2,128)(2,1)S(1)} all-to-all(bf16[64,9,2,128]{3,2,1,0:T(2,128)(2,1)S(1)} %bitcast.12), channel_id=1, replica_groups=mesh['y'=8,'z'=8,'c'=2,'pair'=4] {'y','z'}, dimensions={0} | all-to-all | bytes 589824 | tf_op jit(solution)/shard_map/all_to_all | solution.py:248
  34.7 0.3 phase_sum.1
  35.0 9.5 %all_to_all.16.parts = bf16[8,8,512]{2,1,0:T(8,128)(2,1)S(1)} all-to-all(bf16[8,8,512]{2,1,0:T(8,128)(2,1)S(1)} %phase_sum.1), channel_id=1, replica_groups=mesh['y'=8,'z'=8,'c'=2,'pair'=4] {'c','pair'}, dimensions={0} | all-to-all | bytes 131072 | tf_op jit(solution)/shard_map/all_to_all | solution.py:259
  44.5 0.0 copy-done
  44.5 1.2 %product.1 = (f32[16,128]{1,0:T(8,128)}, bf16[2048,128]{1,0:T(8,128)(2,1)S(1)}) custom-call(bf16[8,8,512]{2,1,0:T(8,128)(2,1)S(1)} %all_to_all.16.parts, bf16[4,2,256,256]{3,2,1,0:T(8,128)(2,1)S(1)} %copy-done, s32[8,128]{1,0:T(8,128)S(1)} %get-tuple-element.7.combo), custom_call_target="tpu_custom_call" | custom-call | tf_op jit(solution)/shard_map/product/pallas_call | solution.py:261
  45.7 24.6 %all_to_all.17 = bf16[64,32,128]{2,1,0:T(8,128)(2,1)S(1)} all-to-all(bf16[64,32,128]{2,1,0:T(8,128)(2,1)S(1)} %bitcast.11), channel_id=1, replica_groups=mesh['y'=8,'z'=8,'c'=2,'pair'=4] {'y','z'}, dimensions={0} | all-to-all | bytes 1048576 | tf_op jit(solution)/shard_map/all_to_all | solution.py:278
  70.3 0.8 %place.1 = bf16[8,64,4,128]{3,2,1,0:T(4,128)(2,1)} custom-call(bf16[64,8,4,128]{3,2,1,0:T(4,128)(2,1)S(1)} %bitcast.9), custom_call_target="tpu_custom_call" | custom-call | tf_op jit(solution)/shard_map/place/pallas_call | solution.py:279
Async XLA Ops:
  0.6 43.8 %copy-start = (bf16[4,2,256,256]{3,2,1,0:T(8,128)(2,1)S(1)}, bf16[4,2,256,256]{3,2,1,0:T(8,128)(2,1)}, u32[]{:S(2)}) copy-start(bf16[4,2,256,256]{3,2,1,0:T(8,128)(2,1)} %delta.1) | copy-start | bytes 3145732
